TPU v7x, 128 devices: a whole 4x4x4 slice. The times are simulated.
128 devices in a mesh: ctx: 8 (over z_hi, x), tp: 16 (over z_lo, y, core).
Axes of the slice: x: 4, y: 4, z: 4 (z_hi: 2, z_lo: 2; z = z_hi * 2 + z_lo), core: 2. Of those that a mesh axis runs over, the one named last changes fastest.
Arguments:
- query_gate: bfloat16 [4096, 8192], P('ctx', 'tp'), may hold values from -6 to 6
- key_gate: bfloat16 [4096, 8192], P('ctx', 'tp'), may hold values from -6 to 6
- value_input: bfloat16 [4096, 8192], P('ctx', 'tp'), may hold values from -6 to 6
- filter_taps: float32 [4096, 512], P('ctx', 'tp'), may hold values from -6 to 6
- out_weight: bfloat16 [8192, 8192], P('tp'), may hold values from -0.09375 to 0.09375
- out_grad: bfloat16 [4096, 8192], P('ctx', 'tp'), may hold values from -6 to 6
Outputs:
- projected: bfloat16 [4096, 8192], P('ctx', 'tp')
- grad_query: bfloat16 [4096, 8192], P('ctx', 'tp')
- grad_key: bfloat16 [4096, 8192], P('ctx', 'tp')
- grad_value: bfloat16 [4096, 8192], P('ctx', 'tp')
- grad_filter: float32 [4096, 512], P('ctx', 'tp')
All inputs are finite; a program needn't handle non-finite values.
Results may differ from a plain program's by a relative error of at most 0.027.
Values may be sent and summed in bfloat16 or wider, within the bound.
A program may use at most 192 MiB of HBM per device.

v0:
```python
import math

import jax
import jax.numpy as jnp
from jax import lax
from jax.sharding import PartitionSpec as P

PRECISE = lax.Precision.HIGHEST


def passed_along(array, axis, by):
    size = lax.axis_size(axis)
    pairs = [(i, i + by) for i in range(size) if 0 <= i + by < size]
    return lax.ppermute(array, axis, pairs)


def basis_tables(length):
    fft_len = 2 * length
    row_ids = jnp.arange(fft_len, dtype=jnp.int32)
    freq_ids = jnp.where(row_ids <= length, row_ids, row_ids - length)
    phase_ids = freq_ids[:, None] * row_ids[None, :] % fft_len
    angles = phase_ids.astype(jnp.float32) * jnp.float32(2.0 * math.pi / fft_len)
    basis = jnp.where((row_ids > length)[:, None], -jnp.sin(angles), jnp.cos(angles))
    inv_weight = jnp.where(
        (row_ids == 0) | (row_ids == length), 1.0 / fft_len, 2.0 / fft_len
    ).astype(jnp.float32)
    pad_basis = basis[:, :length]
    tail_basis = basis[:, length:]
    back_basis = inv_weight[:, None] * tail_basis
    return (pad_basis, tail_basis, back_basis)


def split_basis(basis):
    upper = basis.astype(jnp.bfloat16)
    rest = basis - upper.astype(jnp.float32)
    middle = rest.astype(jnp.bfloat16)
    lower = (rest - middle.astype(jnp.float32)).astype(jnp.bfloat16)
    return (upper, middle, lower)


def split_apply(parts, form, data):
    total = jnp.einsum(form, parts[0], data, preferred_element_type=jnp.float32)
    total = total + jnp.einsum(form, parts[1], data, preferred_element_type=jnp.float32)
    return total + jnp.einsum(form, parts[2], data, preferred_element_type=jnp.float32)


def first_mask(spectrum):
    half_len = spectrum.shape[0] // 2
    return (jnp.arange(half_len) == 0).reshape((half_len,) + (1,) * (spectrum.ndim - 1))


def spec_product(left_spec, right_spec):
    half_len = left_spec.shape[0] // 2
    at_first = first_mask(left_spec)
    left_re = left_spec[:half_len]
    left_im = left_spec[half_len:]
    right_re = right_spec[:half_len]
    right_im = right_spec[half_len:]
    im_product = left_im * right_im
    real_part = left_re * right_re - jnp.where(at_first, 0.0, im_product)
    imag_part = jnp.where(at_first, im_product, left_re * right_im + left_im * right_re)
    return jnp.concatenate([real_part, imag_part], axis=0)


def conjugate(spectrum):
    half_len = spectrum.shape[0] // 2
    imag_half = spectrum[half_len:]
    return jnp.concatenate(
        [spectrum[:half_len], jnp.where(first_mask(spectrum), imag_half, -imag_half)], axis=0
    )


def local(query_gate, key_gate, value_input, filter_taps, out_weight, out_grad):
    length, channels = query_gate.shape
    groups = filter_taps.shape[1]
    per_group = channels // groups
    members = lax.axis_size("ctx")
    position = lax.axis_index("ctx")
    fft_len = 2 * length
    tap_scale = 1.0 / math.sqrt(length * members)
    pad_basis, tail_basis, back_basis = basis_tables(length)
    pad_parts = split_basis(pad_basis)
    back_parts = split_basis(back_basis)
    tap_rows = filter_taps * tap_scale
    product_in = (key_gate.astype(jnp.float32) * value_input.astype(jnp.float32)).astype(
        jnp.bfloat16
    )
    dgated = jnp.einsum(
        "tk,ck->tc",
        lax.all_gather(out_grad, "tp", axis=1, tiled=True),
        out_weight,
        preferred_element_type=jnp.float32,
    ).astype(jnp.bfloat16)
    conv_grad = (dgated.astype(jnp.float32) * query_gate.astype(jnp.float32)).astype(jnp.bfloat16)
    all_taps = (
        lax.all_gather(tap_rows.astype(jnp.bfloat16), "ctx", axis=0, tiled=True)
        .astype(tap_rows.dtype)
        .reshape(members, length, groups)
    )
    own_part = jnp.einsum("nl,dlg->dng", tail_basis, all_taps, precision=PRECISE)
    early_part = jnp.einsum("nl,dlg->dng", pad_basis, all_taps, precision=PRECISE)
    early_part = jnp.concatenate(
        [jnp.zeros((1, fft_len, groups), jnp.float32), early_part[:-1]], axis=0
    )
    spectra = own_part + early_part
    full_spectra = jnp.repeat(spectra, per_group, axis=2)
    spec_in = split_apply(pad_parts, "nl,lc->nc", product_in)
    spec_grad = split_apply(back_parts, "nl,lc->nc", conv_grad)

    def group_total(spectrum):
        return spectrum.reshape(fft_len, groups, per_group).sum(axis=2)

    def visit(totals, spectrum, item_pos):
        fwd_acc, bwd_acc, grad_acc = totals
        distance = jnp.minimum(jnp.abs(position - item_pos), members - 1)
        earlier = (item_pos < position).astype(jnp.float32)
        later_side = (item_pos > position).astype(jnp.float32)
        filter_spec = lax.dynamic_index_in_dim(full_spectra, distance, 0, keepdims=False)
        fwd_acc = fwd_acc + earlier * spec_product(filter_spec, spectrum)
        bwd_acc = bwd_acc + later_side * spec_product(conjugate(filter_spec), spectrum)
        grad_term = earlier * group_total(spec_product(conjugate(spectrum), spec_grad))
        grad_row = lax.dynamic_index_in_dim(grad_acc, distance, 0, keepdims=False)
        grad_acc = lax.dynamic_update_index_in_dim(grad_acc, grad_row + grad_term, distance, 0)
        return (fwd_acc, bwd_acc, grad_acc)

    def from_tokens(forward_part, backward_part, earlier):
        item_parts = (
            jnp.where(earlier, pad_parts[0], back_parts[0]),
            jnp.where(earlier, pad_parts[1], back_parts[1]),
            jnp.where(earlier, pad_parts[2], back_parts[2]),
        )
        item_data = jnp.where(earlier, forward_part, backward_part)
        return split_apply(item_parts, "nl,lc->nc", item_data)

    start_totals = (
        jnp.zeros((fft_len, channels), jnp.float32),
        jnp.zeros((fft_len, channels), jnp.float32),
        jnp.zeros((members, fft_len, groups), jnp.float32),
    )
    received = (
        lax.all_gather(product_in, "ctx", axis=0, tiled=True),
        lax.all_gather(conv_grad, "ctx", axis=0, tiled=True),
    )
    item_count = received[0].shape[0] // length

    def visit_item(item_no, inner):
        forward_part = lax.dynamic_slice_in_dim(received[0], item_no * length, length, 0)
        backward_part = lax.dynamic_slice_in_dim(received[1], item_no * length, length, 0)
        return visit(inner, from_tokens(forward_part, backward_part, item_no < position), item_no)

    totals = lax.fori_loop(0, item_count, visit_item, start_totals)
    fwd_acc, bwd_acc, grad_acc = totals
    own_filter = full_spectra[0]
    fwd_acc = fwd_acc + spec_product(own_filter, spec_in)
    bwd_acc = bwd_acc + spec_product(conjugate(own_filter), spec_grad)
    own_grad = group_total(spec_product(conjugate(spec_in), spec_grad))
    grad_acc = grad_acc.at[0].add(own_grad)
    convolved = jnp.einsum("nl,nc->lc", back_basis, fwd_acc, precision=PRECISE)
    input_grad = jnp.einsum("nl,nc->lc", pad_basis, bwd_acc, precision=PRECISE)
    offset_grad = lax.psum_scatter(
        grad_acc.astype(jnp.bfloat16), "ctx", scatter_dimension=0, tiled=True
    ).astype(jnp.float32)[0]
    own_rows = jnp.einsum("nl,ng->lg", tail_basis, offset_grad, precision=PRECISE)
    early_rows = jnp.einsum("nl,ng->lg", pad_basis, offset_grad, precision=PRECISE)
    later_rows = passed_along(early_rows.astype(jnp.bfloat16), "ctx", -1).astype(early_rows.dtype)
    grad_filter = (own_rows + later_rows) * tap_scale
    gated_out = (query_gate.astype(jnp.float32) * convolved).astype(jnp.bfloat16)
    partial_value = jnp.dot(gated_out, out_weight, preferred_element_type=jnp.float32)
    projected = lax.psum_scatter(
        partial_value.astype(jnp.bfloat16), "tp", scatter_dimension=1, tiled=True
    )
    grad_query = (dgated.astype(jnp.float32) * convolved).astype(jnp.bfloat16)
    grad_key = (input_grad * value_input.astype(jnp.float32)).astype(jnp.bfloat16)
    grad_value = (input_grad * key_gate.astype(jnp.float32)).astype(jnp.bfloat16)
    return (projected, grad_query, grad_key, grad_value, grad_filter)


def solution(mesh):
    return jax.shard_map(
        local,
        mesh=mesh,
        in_specs=(
            P("ctx", "tp"),
            P("ctx", "tp"),
            P("ctx", "tp"),
            P("ctx", "tp"),
            P("tp", None),
            P("ctx", "tp"),
        ),
        out_specs=(P("ctx", "tp"), P("ctx", "tp"), P("ctx", "tp"), P("ctx", "tp"), P("ctx", "tp")),
        check_vma=False,
    )
```

profile of v0, /device:TPU:0, one launch (start us, length us, event | category | flops | bytes accessed | tf_op | source)
XLA Modules:
  0.0 633.0 jit_solution(1408079636187696889)
XLA Ops:
  8.0 2.1 fusion.54
  10.2 54.2 %all-gather.6.cloned.1.call-done = bf16[512,8192]{1,0:T(8,128)(2,1)} async-done(((bf16[512,512]{1,0:T(8,128)(2,1)}), bf16[512,8192]{1,0:T(8,128)(2,1)}) %all-gather.6.cloned.1.call-update) | async-done | bytes 8388624 | tf_op jit(solution)/shard_map/all_gather | solution.py:90
  64.3 11.3 %fusion.56 = (bf16[512,512]{1,0:T(8,128)(2,1)}, bf16[512,512]{1,0:T(8,128)(2,1)}) fusion(bf16[512,512]{1,0:T(8,128)(2,1)S(1)} %copy-done.20, bf16[512,8192]{1,0:T(8,128)(2,1)} %all-gather.6.cloned.1.call-done, bf16[512,8192]{1,0:T(8,128)(2,1)} %param.14), kind=kOutput, calls=%fused_computation.96 | convolution fusion | flops 4296278016 | bytes 18350080 | tf_op jit(solution)/shard_map/tk,ck->tc/dot_general | solution.py:88
  75.7 35.4 %all_gather.12 = bf16[4096,32]{0,1:T(8,128)(2,1)S(1)} all-gather(bf16[512,32]{0,1:T(8,128)(2,1)S(1)} %multiply_convert_fusion), channel_id=1, replica_groups=mesh['ctx'=8,'tp'=16] {'ctx'}, dimensions={0}, use_global_device_ids=true | all-gather | bytes 294912 | tf_op jit(solution)/shard_map/all_gather | solution.py:96
  111.1 17.1 %cosine_select_fusion = f32[1024,1024]{1,0:T(8,128)S(1)} fusion(s32[1024]{0:T(1024)S(1)} %compare_select_fusion, pred[1024]{0:T(1024)(128)(4,1)S(1)} %iota_compare_fusion.3), kind=kLoop, calls=%fused_computation.43 | loop fusion | flops 16777216 | bytes 4199424 | tf_op jit(solution)/shard_map/jit(_where)/select_n | solution.py:23
  135.3 5.4 subtract_convert_fusion
  151.4 3.1 select_subtract_fusion.3
  156.1 2.9 copy.39
  161.1 51.7 %all-gather.8.cloned.1.call-done = bf16[4096,512]{1,0:T(8,128)(2,1)} async-done(((bf16[512,512]{1,0:T(8,128)(2,1)}), bf16[4096,512]{1,0:T(8,128)(2,1)}) %all-gather.8.cloned.1.call-update) | async-done | bytes 4194320 | tf_op jit(solution)/shard_map/all_gather | solution.py:142
  212.8 7.9 %broadcast_in_dim.188 = f32[8,1024,32,16]{1,3,2,0:T(8,128)} broadcast(f32[8,1024,32]{1,2,0:T(8,128)S(1)} %copy-done.14), dimensions={0,1,2} | broadcast | bytes 17825792 | tf_op jit(solution)/shard_map/broadcast_in_dim | solution.py:106
  221.8 238.6 %while.19 = (s32[]{:T(128)}, f32[1024,512]{1,0:T(8,128)}, f32[1024,512]{1,0:T(8,128)}, f32[8,1024,32]{1,2,0:T(8,128)}, s32[]{:T(128)}, /*index=5*/f32[8,1024,512...) while((s32[]{:T(128)}, f32[1024,512]{1,0:T(8,128)}, ...), condition=%wide.region_2.3_spmd.clone, body=%wide.region_0.2_spmd.clone.sunk | while | flops 1625588224 | bytes 89654848 | solution.py:151
  227.4 2.7 constant_dynamic-slice_fusion.3
  230.1 2.5 copy.55
  234.0 5.8 select_subtract_fusion.7
  239.8 5.0 fusion.116
  246.8 2.1 bitcast_reduce_fusion.3
  250.5 2.1 dynamic-slice_select_fusion.2
  256.1 2.7 constant_dynamic-slice_fusion.3
  258.8 2.5 copy.55
  262.7 5.8 select_subtract_fusion.7
  268.5 6.3 fusion.116
  276.8 2.1 bitcast_reduce_fusion.3
  280.5 2.1 dynamic-slice_select_fusion.2
  286.1 2.7 constant_dynamic-slice_fusion.3
  288.8 2.5 copy.55
  292.7 5.8 select_subtract_fusion.7
  298.5 6.3 fusion.116
  306.8 2.1 bitcast_reduce_fusion.3
  310.5 2.1 dynamic-slice_select_fusion.2
  316.1 2.7 constant_dynamic-slice_fusion.3
  318.8 2.5 copy.55
  322.7 5.8 select_subtract_fusion.7
  328.5 6.3 fusion.116
  336.8 2.1 bitcast_reduce_fusion.3
  340.5 2.1 dynamic-slice_select_fusion.2
  346.1 2.7 constant_dynamic-slice_fusion.3
  348.8 2.5 copy.55
  352.6 5.8 select_subtract_fusion.7
  358.4 6.3 fusion.116
  366.8 2.1 bitcast_reduce_fusion.3
  370.5 2.1 dynamic-slice_select_fusion.2
  376.1 2.7 constant_dynamic-slice_fusion.3
  378.8 2.5 copy.55
  382.6 5.8 select_subtract_fusion.7
  388.4 6.3 fusion.116
  396.8 2.1 bitcast_reduce_fusion.3
  400.5 2.1 dynamic-slice_select_fusion.2
  406.1 2.7 constant_dynamic-slice_fusion.3
  408.8 2.5 copy.55
  412.6 5.8 select_subtract_fusion.7
  418.4 6.3 fusion.116
  426.8 2.1 bitcast_reduce_fusion.3
  436.1 2.7 constant_dynamic-slice_fusion.3
  438.8 2.5 copy.55
  442.6 5.8 select_subtract_fusion.7
  448.4 6.3 fusion.116
  456.8 2.1 bitcast_reduce_fusion.3
  462.2 2.1 convert_element_type.211
  464.6 7.0 %fusion.57 = (bf16[512,512]{1,0:T(8,128)(2,1)}, f32[512,512]{1,0:T(8,128)S(1)}) fusion(bf16[512,512]{1,0:T(8,128)(2,1)} %get-tuple-element.412, f32[1024,512]{1,0:T(8,128)S(1)} %copy-done.5, f32[512,512]{1,0:T(8,128)} %get-tuple-element.403, f32[512,512]{1,0:T(8,128)} %get-tuple-element.404, f32[1024,1024]{1,0:T(8,128)} %copy-done, f32[1024]{0:T(1024)S(1)} %fusion.70), kind=kOutput, calls=%fused_computation.97 | convolution fusion | flops 3223584768 | bytes 8392704 | tf_op jit(solution)/shard_map/nl,nc->lc/dot_general | solution.py:158
  471.6 10.1 %convolution_convert_fusion = bf16[512,8192]{1,0:T(8,128)(2,1)} fusion(bf16[512,8192]{1,0:T(8,128)(2,1)} %param.14, f32[512,512]{1,0:T(8,128)S(1)} %get-tuple-element.414, bf16[512,512]{1,0:T(8,128)(2,1)S(1)} %copy-done.21), kind=kOutput, calls=%fused_computation.36 | convolution fusion | flops 4299948032 | bytes 18350080 | tf_op jit(solution)/shard_map/dot_general | solution.py:168
  481.7 67.7 %reduce-scatter.5.cloned.1.call-done = bf16[1,1024,32]{1,2,0:T(8,128)(2,1)} async-done(((bf16[8,1024,32]{1,2,0:T(8,128)(2,1)}), bf16[1,1024,32]{1,2,0:T(8,128)(2,1)}) %reduce-scatter.5.cloned.1.call-update) | async-done | bytes 65552 | tf_op jit(solution)/shard_map/reduce_scatter | solution.py:160
  549.4 2.4 fusion.49
  553.2 6.8 %fusion.53 = (bf16[512,512]{1,0:T(8,128)(2,1)}, bf16[512,512]{1,0:T(8,128)(2,1)}) fusion(bf16[512,512]{1,0:T(8,128)(2,1)} %param.11, bf16[512,512]{1,0:T(8,128)(2,1)} %param.12, f32[1024,512]{1,0:T(8,128)S(1)} %copy-done.6, f32[512,512]{1,0:T(8,128)S(1)} %copy-done.17, f32[512,512]{1,0:T(8,128)} %get-tuple-element.406, f32[1024,1024]{1,0:T(8,128)} %copy-done), kind=kOutput, calls=%fused_computation.93 | convolution fusion | flops 3223846912 | bytes 8388608 | tf_op jit(solution)/shard_map/nl,nc->lc/dot_general | solution.py:159
  561.5 64.8 %reduce-scatter.3.cloned.1.call-done = bf16[512,512]{1,0:T(8,128)(2,1)} async-done(((bf16[512,8192]{1,0:T(8,128)(2,1)}), bf16[512,512]{1,0:T(8,128)(2,1)}) %reduce-scatter.3.cloned.1.call-update) | async-done | bytes 524304 | tf_op jit(solution)/shard_map/reduce_scatter | solution.py:169
  (233 shorter events, 99.2 us)
Async XLA Ops:
  7.2 57.2 %copy-start.20 = (bf16[512,512]{1,0:T(8,128)(2,1)S(1)}, bf16[512,512]{1,0:T(8,128)(2,1)}, u32[]{:S(2)}) copy-start(bf16[512,512]{1,0:T(8,128)(2,1)} %param.10) | copy-start | bytes 1572868
  7.2 57.2 %all-gather.6.cloned.1.call-start = ((), (), s32[]{:S(2)}) async-start(), calls=%async_computation.3 | async-start | bytes 8912896 | tf_op jit(solution)/shard_map/all_gather | solution.py:90
  7.9 153.2 %all-gather.4.cloned.1.call-start = ((), (), s32[]{:S(2)}) async-start(), calls=%async_computation.2 | async-start | bytes 4718592 | tf_op jit(solution)/shard_map/all_gather | solution.py:141
  10.1 65.6 %copy-start.19 = (f32[512,32]{0,1:T(8,128)S(1)}, f32[512,32]{0,1:T(8,128)}, u32[]{:S(2)}) copy-start(f32[512,32]{0,1:T(8,128)} %param.13) | copy-start | bytes 196612
  10.1 202.7 %all-gather.8.cloned.1.call-start = ((), (), s32[]{:S(2)}) async-start(), calls=%async_computation.4 | async-start | bytes 4718592 | tf_op jit(solution)/shard_map/all_gather | solution.py:142
  75.6 473.8 %reduce-scatter.5.cloned.1.call-start = ((), (), s32[]{:S(2)}) async-start(), calls=%async_computation.6 | async-start | bytes 589824 | tf_op jit(solution)/shard_map/reduce_scatter | solution.py:160
  135.3 5.4 copy-start.11
  159.0 53.8 %copy-start.14 = (f32[8,1024,32]{1,2,0:T(8,128)S(1)}, f32[8,1024,32]{1,2,0:T(8,128)}, u32[]{:S(2)}) copy-start(f32[8,1024,32]{1,2,0:T(8,128)} %copy-done.13) | copy-start | bytes 3145732
  221.8 4.0 copy-start.9
  221.8 4.8 copy-start.7
  239.8 5.0 copy-start.2
  239.8 5.0 copy-start.3
  246.8 3.7 copy-start.8
  246.8 3.7 copy-start.10
  250.5 4.1 copy-start.9
  250.5 4.8 copy-start.7
  268.5 6.3 copy-start.2
  268.5 6.3 copy-start.3
  276.8 3.7 copy-start.8
  276.8 3.7 copy-start.10
  280.5 4.1 copy-start.9
  280.5 4.8 copy-start.7
  298.4 6.3 copy-start.2
  298.4 6.3 copy-start.3
  306.8 3.7 copy-start.8
  306.8 3.7 copy-start.10
  310.5 4.1 copy-start.9
  310.5 4.8 copy-start.7
  328.5 6.3 copy-start.2
  328.5 6.3 copy-start.3
  336.8 3.7 copy-start.8
  336.8 3.7 copy-start.10
  340.5 4.1 copy-start.9
  340.5 4.8 copy-start.7
  358.4 6.3 copy-start.2
  358.4 6.3 copy-start.3
  366.8 3.7 copy-start.8
  366.8 3.7 copy-start.10
  370.5 4.1 copy-start.9
  370.5 4.8 copy-start.7
  388.4 6.3 copy-start.2
  388.4 6.3 copy-start.3
  396.8 3.7 copy-start.8
  396.8 3.7 copy-start.10
  400.5 4.1 copy-start.9
  400.5 4.8 copy-start.7
  418.4 6.3 copy-start.2
  418.4 6.3 copy-start.3
  426.8 3.7 copy-start.8
  426.8 3.7 copy-start.10
  430.5 4.1 copy-start.9
  430.5 4.8 copy-start.7
  448.4 6.3 copy-start.2
  448.4 6.3 copy-start.3
  456.7 3.7 copy-start.8
  456.8 3.7 copy-start.10
  460.5 4.1 copy-start.5
  464.3 161.9 %reduce-scatter.3.cloned.1.call-start = ((), (), s32[]{:S(2)}) async-start(), calls=%async_computation.5 | async-start | bytes 8912896 | tf_op jit(solution)/shard_map/reduce_scatter | solution.py:169
  464.6 7.0 %copy-start.21 = (bf16[512,512]{1,0:T(8,128)(2,1)S(1)}, bf16[512,512]{1,0:T(8,128)(2,1)}, u32[]{:S(2)}) copy-start(bf16[512,512]{1,0:T(8,128)(2,1)} %param.10) | copy-start | bytes 1572868
  481.7 71.4 %copy-start.17 = (f32[512,512]{1,0:T(8,128)S(1)}, f32[512,512]{1,0:T(8,128)}, u32[]{:S(2)}) copy-start(f32[512,512]{1,0:T(8,128)} %get-tuple-element.405) | copy-start | bytes 3145732
  481.7 71.4 %copy-start.6 = (f32[1024,512]{1,0:T(8,128)S(1)}, f32[1024,512]{1,0:T(8,128)}, u32[]{:S(2)}) copy-start(f32[1024,512]{1,0:T(8,128)} %get-tuple-element.264) | copy-start | bytes 6291460
  551.8 8.2 %collective-permute-start = (bf16[512,32]{0,1:T(8,128)(2,1)S(1)}, bf16[512,32]{0,1:T(8,128)(2,1)S(1)}, u32[]{:S(2)}, u32[]{:S(2)}) collective-permute-start(bf16[512,32]{0,1:T(8,128)(2,1)S(1)} %fusion.49), channel_id=1, source_target_pairs={{16,0},{32,16},{48,32},{64,48},{80,64},{96,80},{112,96},{17,1},{33... | collective-permute-start | bytes 98312 | tf_op jit(solution)/shard_map/ppermute | solution.py:14
  553.2 6.9 %copy-start.1 = (f32[1024,1024]{1,0:T(8,128)S(1)}, f32[1024,1024]{1,0:T(8,128)}, u32[]{:S(2)}) copy-start(f32[1024,1024]{1,0:T(8,128)} %copy-done) | copy-start | bytes 12582916
  553.2 6.9 %copy-start.18 = (bf16[1,1024,32]{1,2,0:T(8,128)(2,1)S(1)}, bf16[1,1024,32]{1,2,0:T(8,128)(2,1)}, u32[]{:S(2)}) copy-start(bf16[1,1024,32]{1,2,0:T(8,128)(2,1)} %reduce-scatter.5.cloned.1.call-done) | copy-start | bytes 196612
  (6 other events, 11.1 us)
Sparse Core Ops, SparseCore 0:
  9.7 54.6 all-gather.5
  67.2 73.2 all-gather.3
  143.5 69.2 all-gather.7
  464.5 84.9 reduce-scatter.4
  552.4 73.8 reduce-scatter.2
where the time goes:
time: 639 us; the launch traced here: 633 us
  waiting for transfers between devices  239 us (37%)
  other arithmetic  179 us (28%)
  local copies, waits for them, and re-layouts  84.6 us (13%)
  matrix products  78.7 us (12%)
  blocking collectives  35.4 us (6%)
  between operations  14.3 us (2%)
    reduce_scatter x1, waiting for transfers between devices, local(): lax.psum_scatter(grad_acc.astype(jnp.bfloat16), 'ctx', scatter_dimension=...  67.7 us
    reduce_scatter x1, waiting for transfers between devices, local(): lax.psum_scatter(partial_value.astype(jnp.bfloat16), 'tp', scatter_dimens...  64.8 us
    all_gather x1, waiting for transfers between devices, local(): lax.all_gather(out_grad, 'tp', axis=1, tiled=True)  54.2 us
    all_gather x1, waiting for transfers between devices, local(): lax.all_gather(conv_grad, 'ctx', axis=0, tiled=True)  51.7 us
    sub x9, other arithmetic, spec_product(): real_part = left_re * right_re - jnp.where(at_first, 0.0, im_product)  49.5 us
    add x8, other arithmetic, visit(): fwd_acc = fwd_acc + earlier * spec_product(filter_spec, spectrum)  49.2 us
    all_gather x1, blocking collectives, local(): lax.all_gather(tap_rows.astype(jnp.bfloat16), 'ctx', axis=0, tiled=True)  35.4 us
    while x112, local copies, waits for them, and re-layouts  31 us
  transfers between devices with their start and end apart: 6, of which 4 were waited for; matrix products, arithmetic and copies ran while one was open for 14% of the time, Pallas kernels for 0%

commit v1 on v0

v1 whole, which is shorter than its diff:
```python
import math

import jax
import jax.numpy as jnp
from jax import lax
from jax.experimental import pallas as pl
from jax.experimental.pallas import tpu as pltpu
from jax.sharding import PartitionSpec as P

B=256; H=128
def build_tb(tb_ref, g, taps_row):
    L=taps_row.shape[1]
    z=jnp.zeros((1,H),jnp.float32)
    v=jnp.broadcast_to(jnp.concatenate([z,taps_row,z],axis=1),(16,L+2*H))
    base=pltpu.roll(v,0,1,stride=1,stride_axis=0)
    for k in range(H//16):
        r=pltpu.roll(base,16*k,1) if k else base
        tb_ref[g,16*k:16*k+16,:]=r.astype(jnp.bfloat16)
def tmat(tb_ref,g):
    L=tb_ref.shape[2]-2*H
    return jnp.concatenate([tb_ref[g,:,H:H+L],tb_ref[g,:,0:L]],axis=0)
def conv_fwd(xp_ref, tb_ref, g):
    R=xp_ref.shape[1]//2; nb=R//16
    acc=None
    xs=[xp_ref[g,R-16*d:2*R-16*d,:] for d in range(nb)]
    ts=[jnp.concatenate([tb_ref[g,:,H+B*d:H+B*d+B],tb_ref[g,:,B*d:B*d+B]],axis=0) for d in range(nb)]
    return jnp.dot(jnp.concatenate(xs,axis=1),jnp.concatenate(ts,axis=0),preferred_element_type=jnp.float32)
def gg_of(gp_ref,g):
    R=gp_ref.shape[1]//2; nb=R//16
    return jnp.concatenate([gp_ref[g,16*d:16*d+R,:] for d in range(nb)],axis=1)
def conv_bwd(gg, t):
    return lax.dot_general(gg,t,(((1,),(1,)),((),())),preferred_element_type=jnp.float32)
def filt_grad(x, gg):
    C=lax.dot_general(x,gg,(((0,),(0,)),((),())),preferred_element_type=jnp.float32)
    L=C.shape[1]
    z=jnp.zeros((H,H),jnp.float32)
    top=C[:H]; bot=jnp.concatenate([C[H:,H:],z],axis=1)
    D=top+bot
    n=H
    D=jnp.concatenate([D,z],axis=1)
    W=L+H
    lane=None
    while n>1:
        n//=2
        D=D[:n]+pltpu.roll(D[n:],W-n,1)
    return D[:,:L]


VM = pl.BlockSpec(memory_space=pltpu.VMEM)
PARAMS = pltpu.CompilerParams(vmem_limit_bytes=56 << 20)


def k_fwd(taps_ref, x_ref, y_ref, tb_ref, xp):
    G, R, _ = x_ref.shape
    xp[:, :R, :] = jnp.zeros((G, R, B), jnp.bfloat16)
    xp[:, R:, :] = x_ref[...]
    for g in range(G):
        build_tb(tb_ref, g, taps_ref[g : g + 1, :])

    def body(g, _):
        y_ref[g] = conv_fwd(xp, tb_ref, g).astype(jnp.bfloat16)
        return 0

    lax.fori_loop(0, G, body, 0)


def k_bwd(tb_ref, x_ref, g_ref, u_ref, f_ref, gp):
    G, R, _ = x_ref.shape
    gp[:, R:, :] = jnp.zeros((G, R, B), jnp.bfloat16)
    gp[:, :R, :] = g_ref[...]

    def body(g, _):
        gg = gg_of(gp, g)
        u_ref[g] = conv_bwd(gg, tmat(tb_ref, g)).astype(jnp.bfloat16)
        f_ref[g] = filt_grad(x_ref[g], gg)
        return 0

    lax.fori_loop(0, G, body, 0)


def local(query_gate, key_gate, value_input, filter_taps, out_weight, out_grad):
    length, channels = query_gate.shape
    groups = filter_taps.shape[1]
    per = channels // groups
    n = lax.axis_size("ctx")
    G = groups // n
    nb = length // B
    total = n * length
    R = n * nb * per
    scale = 1.0 / math.sqrt(total)
    f32 = jnp.float32
    bf = jnp.bfloat16

    def scatter(v):
        v = v.T.reshape(n, G * per, length)
        v = lax.all_to_all(v, "ctx", 0, 0, tiled=True)
        v = v.reshape(n, G, per, nb, B).transpose(1, 0, 3, 2, 4)
        return v.reshape(G, R, B)

    def gather(v):
        v = v.reshape(G, n, nb, per, B).transpose(1, 0, 3, 2, 4).reshape(n, G * per, length)
        v = lax.all_to_all(v, "ctx", 0, 0, tiled=True)
        return v.reshape(channels, length).T

    product_in = (key_gate.astype(f32) * value_input.astype(f32)).astype(bf)
    taps = (filter_taps * scale).T.reshape(n, G, length)
    taps = lax.all_to_all(taps, "ctx", 0, 0, tiled=True)
    taps = taps.transpose(1, 0, 2).reshape(G, total)
    x = scatter(product_in)
    y, tb = pl.pallas_call(
        k_fwd,
        in_specs=[VM] * 2,
        out_specs=(VM, VM),
        out_shape=(
            jax.ShapeDtypeStruct((G, R, B), bf),
            jax.ShapeDtypeStruct((G, H, total + 2 * H), bf),
        ),
        scratch_shapes=[pltpu.VMEM((G, 2 * R, B), bf)],
        compiler_params=PARAMS,
    )(taps, x)
    convolved = gather(y).astype(f32)
    gated_out = (query_gate.astype(f32) * convolved).astype(bf)
    partial_value = jnp.dot(gated_out, out_weight, preferred_element_type=f32)
    projected = lax.psum_scatter(partial_value.astype(bf), "tp", scatter_dimension=1, tiled=True)
    dgated = jnp.einsum(
        "tk,ck->tc",
        lax.all_gather(out_grad, "tp", axis=1, tiled=True),
        out_weight,
        preferred_element_type=f32,
    ).astype(bf).astype(f32)
    conv_grad = (dgated * query_gate.astype(f32)).astype(bf)
    gg = scatter(conv_grad)
    u, fg = pl.pallas_call(
        k_bwd,
        in_specs=[VM] * 3,
        out_specs=(VM, VM),
        out_shape=(
            jax.ShapeDtypeStruct((G, R, B), bf),
            jax.ShapeDtypeStruct((G, 1, total), f32),
        ),
        scratch_shapes=[pltpu.VMEM((G, 2 * R, B), bf)],
        compiler_params=PARAMS,
    )(tb, x, gg)
    input_grad = gather(u).astype(f32)
    fg = fg.reshape(G, n, length).transpose(1, 0, 2)
    fg = lax.all_to_all(fg, "ctx", 0, 0, tiled=True).reshape(groups, length)
    grad_filter = fg.T * scale
    grad_query = (dgated * convolved).astype(bf)
    grad_key = (input_grad * value_input.astype(f32)).astype(bf)
    grad_value = (input_grad * key_gate.astype(f32)).astype(bf)
    return (projected, grad_query, grad_key, grad_value, grad_filter)


def solution(mesh):
    spec = P("ctx", "tp")
    return jax.shard_map(
        local,
        mesh=mesh,
        in_specs=(spec, spec, spec, spec, P("tp", None), spec),
        out_specs=(spec,) * 5,
        check_vma=False,
    )
```

time: 639 us -> 167 us (0.26)
  waiting for transfers between devices: 239 us -> 51.1 us
  other arithmetic: 179 us -> 3.7 us
  local copies, waits for them, and re-layouts: 84.6 us -> 15.1 us
  matrix products: 78.7 us -> 20.6 us
  starting transfers between devices: 1.67 us -> 21.8 us
  Pallas kernels: 0 us -> 17.4 us
  blocking collectives: 35.4 us -> 20.4 us
    reduce_scatter x2 -> x1, waiting for transfers between devices: 132 us -> 2.77 us  [local(): lax.psum_scatter(partial_value.astype(bf), 'tp', scatter_dimension=1, til...]
    dot_general x37 -> x1, matrix products: 67.5 us -> 10.2 us  [local(): partial_value = jnp.dot(gated_out, out_weight, preferred_element_type=f32)]
    all_gather x1, waiting for transfers between devices: 54.2 us -> 0.02 us  [local(): lax.all_gather(out_grad, 'tp', axis=1, tiled=True)]
    all_gather x2 -> x0, waiting for transfers between devices: 51.7 us -> none  [the longest x1 51.7 us: local(): lax.all_gather(conv_grad, 'ctx', axis=0, tiled=True)]
    sub x9 -> x0, other arithmetic: 49.5 us -> none  [spec_product(): real_part = left_re * right_re - jnp.where(at_first, 0.0, im_product)]
    add x8 -> x0, other arithmetic: 49.2 us -> none  [visit(): fwd_acc = fwd_acc + earlier * spec_product(filter_spec, spectrum)]
    all_to_all x0 -> x5, waiting for transfers between devices: none -> 47.6 us  [the longest x2 25.4 us: gather(): v = lax.all_to_all(v, 'ctx', 0, 0, tiled=True)]
    all_gather x1 -> x0, blocking collectives: 35.4 us -> none  [local(): lax.all_gather(tap_rows.astype(jnp.bfloat16), 'ctx', axis=0, tiled=True)]
  transfers between devices with their start and end apart: 6 -> 7, of which waited for: 4 -> 6; matrix products, arithmetic and copies ran while one was open for 14% -> 24% of each run, Pallas kernels for 0% -> 11%
where the time goes in v1:
time: 167 us; the launch traced here: 164 us
  waiting for transfers between devices  51.1 us (31%)
  starting transfers between devices  21.8 us (13%)
  matrix products  20.6 us (12%)
  blocking collectives  20.4 us (12%)
  Pallas kernels  17.4 us (10%)
  local copies, waits for them, and re-layouts  15.1 us (9%)
  between operations  14.1 us (8%)
  other arithmetic  3.7 us (2%)
    all_to_all x2, waiting for transfers between devices, gather(): v = lax.all_to_all(v, 'ctx', 0, 0, tiled=True)  25.4 us
    all_to_all x1, blocking collectives, scatter(): v = lax.all_to_all(v, 'ctx', 0, 0, tiled=True)  20.4 us
    pallas_call x1, Pallas kernels, local(): pl.pallas_call(k_bwd, in_specs=[VM] * 3, out_specs=(VM, VM), out_shape=(j...  10.4 us
    dot_general x1, matrix products, local(): jnp.einsum('tk,ck->tc', lax.all_gather(out_grad, 'tp', axis=1, tiled=True...  10.3 us
    dot_general x1, matrix products, local(): partial_value = jnp.dot(gated_out, out_weight, preferred_element_type=f32)  10.2 us
    all_to_all x1, waiting for transfers between devices, scatter(): v = lax.all_to_all(v, 'ctx', 0, 0, tiled=True)  10.1 us
    all_to_all x1, starting transfers between devices, scatter(): v = lax.all_to_all(v, 'ctx', 0, 0, tiled=True)  7.7 us
    all_to_all x2, starting transfers between devices, gather(): v = lax.all_to_all(v, 'ctx', 0, 0, tiled=True)  6.99 us
  transfers between devices with their start and end apart: 7, of which 6 were waited for; matrix products, arithmetic and copies ran while one was open for 24% of the time, Pallas kernels for 11%

profile of v1, /device:TPU:0, one launch (start us, length us, event | category | flops | bytes accessed | tf_op | source)
XLA Modules:
  0.0 164.1 jit_solution(3283031348708818091)
XLA Ops:
  7.2 0.0 copy-start
  7.2 0.0 all-gather.2.cloned.1.call-start
  7.2 0.7 all-gather.2.cloned.1.call-update
  7.9 1.3 copy.28
  9.2 1.3 copy.29
  10.4 0.9 fusion.2
  11.4 7.7 %all-to-all-start.1 = ((bf16[8,64,512]{2,1,0:T(8,128)(2,1)}), bf16[8,64,512]{2,1,0:T(8,128)(2,1)S(1)}, u32[]{:S(2)}, u32[]{:S(2)}) async-start(bf16[8,64,512]{2,1,0:T(8,128)(2,1)} %bitcast.4), calls=%async_computation.1 | async-start | bytes 1048576 | tf_op jit(solution)/shard_map/all_to_all | solution.py:96
  19.0 0.8 multiply_bitcast_fusion
  19.9 0.7 reshape.58
  20.5 10.1 %all-to-all-done.1 = bf16[8,64,512]{2,1,0:T(8,128)(2,1)S(1)} async-done(((bf16[8,64,512]{2,1,0:T(8,128)(2,1)}), bf16[8,64,512]{2,1,0:T(8,128)(2,1)S(1)}, u32[]{:S(2)}, u32[]{:S(2)}) %all-to-all-start.1) | async-done | bytes 524320 | tf_op jit(solution)/shard_map/all_to_all | solution.py:96
  30.7 3.5 %all-to-all-start = ((f32[8,4,512]{2,1,0:T(4,128)}), f32[8,4,512]{2,1,0:T(4,128)S(1)}, u32[]{:S(2)}, u32[]{:S(2)}) async-start(f32[8,4,512]{2,1,0:T(4,128)} %reshape.58), calls=%async_computation | async-start | bytes 131072 | tf_op jit(solution)/shard_map/all_to_all | solution.py:107
  34.2 0.1 reshape.61
  34.3 0.9 copy.30
  35.2 6.8 %all-to-all-done = f32[8,4,512]{2,1,0:T(4,128)S(1)} async-done(((f32[8,4,512]{2,1,0:T(4,128)}), f32[8,4,512]{2,1,0:T(4,128)S(1)}, u32[]{:S(2)}, u32[]{:S(2)}) %all-to-all-start) | async-done | bytes 65568 | tf_op jit(solution)/shard_map/all_to_all | solution.py:107
  42.0 0.0 copy-start.1
  42.0 0.6 copy-done.1
  42.7 7.0 %shard_map.101 = (bf16[4,256,256]{2,1,0:T(8,128)(2,1)}, bf16[4,128,4352]{2,1,0:T(8,128)(2,1)}) custom-call(f32[4,4096]{1,0:T(4,128)} %bitcast.61, bf16[4,256,256]{2,1,0:T(8,128)(2,1)} %bitcast.50), custom_call_target="tpu_custom_call" | custom-call | tf_op jit(solution)/shard_map/pallas_call | solution.py:110
  49.6 1.6 copy.41
  51.2 1.1 reshape.64
  52.3 3.5 %all-to-all-start.2 = ((bf16[8,64,512]{2,1,0:T(8,128)(2,1)}), bf16[8,64,512]{2,1,0:T(8,128)(2,1)S(1)}, u32[]{:S(2)}, u32[]{:S(2)}) async-start(bf16[8,64,512]{2,1,0:T(8,128)(2,1)} %reshape.64), calls=%async_computation.2 | async-start | bytes 1048576 | tf_op jit(solution)/shard_map/all_to_all | solution.py:102
  55.8 0.0 reduce-scatter.2.cloned.1.call-start
  55.9 0.0 copy-done
  55.9 0.2 copy.27
  56.1 10.5 %all-to-all-done.2 = bf16[8,64,512]{2,1,0:T(8,128)(2,1)S(1)} async-done(((bf16[8,64,512]{2,1,0:T(8,128)(2,1)}), bf16[8,64,512]{2,1,0:T(8,128)(2,1)S(1)}, u32[]{:S(2)}, u32[]{:S(2)}) %all-to-all-start.2) | async-done | bytes 524320 | tf_op jit(solution)/shard_map/all_to_all | solution.py:102
  66.6 10.2 %convolution_convert_fusion = bf16[512,8192]{1,0:T(8,128)(2,1)} fusion(bf16[512,8192]{1,0:T(8,128)(2,1)} %param.10, bf16[512,512]{0,1:T(8,128)(2,1)S(1)} %copy.27, bf16[512,512]{1,0:T(8,128)(2,1)S(1)} %bitcast.52), kind=kOutput, calls=%fused_computation | convolution fusion | flops 4300210176 | bytes 17825792 | tf_op jit(solution)/shard_map/dot_general | solution.py:123
  76.9 0.0 reduce-scatter.2.cloned.1.call-update
  76.9 0.0 all-gather.2.cloned.1.call-done
  76.9 10.3 %fusion.5 = (bf16[512,512]{0,1:T(8,128)(2,1)S(1)}, bf16[512,512]{0,1:T(8,128)(2,1)S(1)}) fusion(bf16[512,512]{0,1:T(8,128)(2,1)S(1)} %copy.27, bf16[8,64,512]{2,1,0:T(8,128)(2,1)S(1)} %all-to-all-done.2, bf16[512,8192]{1,0:T(8,128)(2,1)} %all-gather.2.cloned.1.call-done, bf16[512,8192]{1,0:T(8,128)(2,1)} %param.10), kind=kOutput, calls=%fused_computation.13 | convolution fusion | flops 4297064448 | bytes 18874368 | tf_op jit(solution)/shard_map/tk,ck->tc/dot_general | solution.py:125
  87.3 20.4 %all_to_all.30 = bf16[8,64,512]{2,1,0:T(8,128)(2,1)S(1)} all-to-all(bf16[8,64,512]{2,1,0:T(8,128)(2,1)S(1)} %bitcast.59), channel_id=1, replica_groups=mesh['ctx'=8,'tp'=16] {'ctx'}, dimensions={0} | all-to-all | bytes 1048576 | tf_op jit(solution)/shard_map/all_to_all | solution.py:96
  107.6 0.1 reshape.66
  107.7 0.9 copy.32
  108.6 10.4 %shard_map.102 = (bf16[4,256,256]{2,1,0:T(8,128)(2,1)}, f32[4,1,4096]{2,1,0:T(1,128)}) custom-call(bf16[4,128,4352]{2,1,0:T(8,128)(2,1)} %get-tuple-element.10.tb_ref, bf16[4,256,256]{2,1,0:T(8,128)(2,1)} %bitcast.51, bf16[4,256,256]{2,1,0:T(8,128)(2,1)} %bitcast.57), custom_call_target="tpu_custom_call" | custom-call | tf_op jit(solution)/shard_map/pallas_call | solution.py:133
  119.1 1.6 reduce
  120.7 3.5 %all-to-all-start.5 = ((f32[8,4,512]{2,1,0:T(4,128)}), f32[8,4,512]{2,1,0:T(4,128)S(1)}, u32[]{:S(2)}, u32[]{:S(2)}) async-start(f32[8,4,512]{2,1,0:T(4,128)} %bitcast.21), calls=%async_computation.6 | async-start | bytes 131072 | tf_op jit(solution)/shard_map/all_to_all | solution.py:146
  124.2 1.6 copy.40
  125.8 1.1 reshape.69
  126.9 5.2 %all-to-all-done.5 = f32[8,4,512]{2,1,0:T(4,128)S(1)} async-done(((f32[8,4,512]{2,1,0:T(4,128)}), f32[8,4,512]{2,1,0:T(4,128)S(1)}, u32[]{:S(2)}, u32[]{:S(2)}) %all-to-all-start.5) | async-done | bytes 65568 | tf_op jit(solution)/shard_map/all_to_all | solution.py:146
  132.2 3.5 %all-to-all-start.4 = ((bf16[8,64,512]{2,1,0:T(8,128)(2,1)}), bf16[8,64,512]{2,1,0:T(8,128)(2,1)S(1)}, u32[]{:S(2)}, u32[]{:S(2)}) async-start(bf16[8,64,512]{2,1,0:T(8,128)(2,1)} %reshape.69), calls=%async_computation.5 | async-start | bytes 1048576 | tf_op jit(solution)/shard_map/all_to_all | solution.py:102
  135.7 1.0 copy.35
  136.7 0.7 mul.38
  137.3 14.8 %all-to-all-done.4 = bf16[8,64,512]{2,1,0:T(8,128)(2,1)S(1)} async-done(((bf16[8,64,512]{2,1,0:T(8,128)(2,1)}), bf16[8,64,512]{2,1,0:T(8,128)(2,1)S(1)}, u32[]{:S(2)}, u32[]{:S(2)}) %all-to-all-start.4) | async-done | bytes 524320 | tf_op jit(solution)/shard_map/all_to_all | solution.py:102
  152.2 0.3 fusion.1
  152.4 1.0 copy.37
  153.5 1.0 copy.36
  154.5 2.8 %reduce-scatter.2.cloned.1.call-done = bf16[512,512]{1,0:T(8,128)(2,1)} async-done(((bf16[512,8192]{1,0:T(8,128)(2,1)}), bf16[512,512]{1,0:T(8,128)(2,1)}) %reduce-scatter.2.cloned.1.call-update) | async-done | bytes 524304 | tf_op jit(solution)/shard_map/reduce_scatter | solution.py:124
  (1 shorter events, 0.0 us)
Async XLA Ops:
  7.2 48.7 %copy-start = (bf16[512,512]{1,0:T(8,128)(2,1)S(1)}, bf16[512,512]{1,0:T(8,128)(2,1)}, u32[]{:S(2)}) copy-start(bf16[512,512]{1,0:T(8,128)(2,1)} %param.6) | copy-start | bytes 1572868
  7.2 69.7 %all-gather.2.cloned.1.call-start = ((), (), s32[]{:S(2)}) async-start(), calls=%async_computation.8 | async-start | bytes 8912896 | tf_op jit(solution)/shard_map/all_gather | solution.py:127
  11.4 19.3 %all-to-all-start.1 = ((bf16[8,64,512]{2,1,0:T(8,128)(2,1)}), bf16[8,64,512]{2,1,0:T(8,128)(2,1)S(1)}, u32[]{:S(2)}, u32[]{:S(2)}) async-start(bf16[8,64,512]{2,1,0:T(8,128)(2,1)} %bitcast.4), calls=%async_computation.1 | async-start | bytes 1048576 | tf_op jit(solution)/shard_map/all_to_all | solution.py:96
  30.7 11.3 %all-to-all-start = ((f32[8,4,512]{2,1,0:T(4,128)}), f32[8,4,512]{2,1,0:T(4,128)S(1)}, u32[]{:S(2)}, u32[]{:S(2)}) async-start(f32[8,4,512]{2,1,0:T(4,128)} %reshape.58), calls=%async_computation | async-start | bytes 131072 | tf_op jit(solution)/shard_map/all_to_all | solution.py:107
  42.0 0.6 copy-start.1
  52.3 14.3 %all-to-all-start.2 = ((bf16[8,64,512]{2,1,0:T(8,128)(2,1)}), bf16[8,64,512]{2,1,0:T(8,128)(2,1)S(1)}, u32[]{:S(2)}, u32[]{:S(2)}) async-start(bf16[8,64,512]{2,1,0:T(8,128)(2,1)} %reshape.64), calls=%async_computation.2 | async-start | bytes 1048576 | tf_op jit(solution)/shard_map/all_to_all | solution.py:102
  55.8 101.4 %reduce-scatter.2.cloned.1.call-start = ((), (), s32[]{:S(2)}) async-start(), calls=%async_computation.7 | async-start | bytes 8912896 | tf_op jit(solution)/shard_map/reduce_scatter | solution.py:124
  120.7 11.5 %all-to-all-start.5 = ((f32[8,4,512]{2,1,0:T(4,128)}), f32[8,4,512]{2,1,0:T(4,128)S(1)}, u32[]{:S(2)}, u32[]{:S(2)}) async-start(f32[8,4,512]{2,1,0:T(4,128)} %bitcast.21), calls=%async_computation.6 | async-start | bytes 131072 | tf_op jit(solution)/shard_map/all_to_all | solution.py:146
  132.2 20.0 %all-to-all-start.4 = ((bf16[8,64,512]{2,1,0:T(8,128)(2,1)}), bf16[8,64,512]{2,1,0:T(8,128)(2,1)S(1)}, u32[]{:S(2)}, u32[]{:S(2)}) async-start(bf16[8,64,512]{2,1,0:T(8,128)(2,1)} %reshape.69), calls=%async_computation.5 | async-start | bytes 1048576 | tf_op jit(solution)/shard_map/all_to_all | solution.py:102
Sparse Core Ops, SparseCore 0:
  9.7 64.4 all-gather.1
  77.1 80.0 reduce-scatter.1

commit v2 on v1

v2 whole, which is shorter than its diff:
```python
import math

import jax
import jax.numpy as jnp
from jax import lax
from jax.experimental import pallas as pl
from jax.experimental.pallas import tpu as pltpu
from jax.sharding import PartitionSpec as P

MESH = pl.DeviceIdType.MESH
f32 = jnp.float32
bf = jnp.bfloat16
B=256; H=128
def build_tb(tb_ref, g, taps_row):
    L=taps_row.shape[1]
    z=jnp.zeros((1,H),jnp.float32)
    v=jnp.broadcast_to(jnp.concatenate([z,taps_row,z],axis=1),(16,L+2*H))
    base=pltpu.roll(v,0,1,stride=1,stride_axis=0)
    for k in range(H//16):
        r=pltpu.roll(base,16*k,1) if k else base
        tb_ref[g,16*k:16*k+16,:]=r.astype(jnp.bfloat16)
def tmat(tb_ref,g):
    L=tb_ref.shape[2]-2*H
    return jnp.concatenate([tb_ref[g,:,H:H+L],tb_ref[g,:,0:L]],axis=0)
def conv_fwd(xp_ref, tb_ref, g):
    R=xp_ref.shape[1]//2; nb=R//16
    acc=None
    xs=[xp_ref[g,R-16*d:2*R-16*d,:] for d in range(nb)]
    ts=[jnp.concatenate([tb_ref[g,:,H+B*d:H+B*d+B],tb_ref[g,:,B*d:B*d+B]],axis=0) for d in range(nb)]
    return jnp.dot(jnp.concatenate(xs,axis=1),jnp.concatenate(ts,axis=0),preferred_element_type=jnp.float32)
def gg_of(gp_ref,g):
    R=gp_ref.shape[1]//2; nb=R//16
    return jnp.concatenate([gp_ref[g,16*d:16*d+R,:] for d in range(nb)],axis=1)
def conv_bwd(gg, t):
    return lax.dot_general(gg,t,(((1,),(1,)),((),())),preferred_element_type=jnp.float32)
def filt_grad(x, gg):
    C=lax.dot_general(x,gg,(((0,),(0,)),((),())),preferred_element_type=jnp.float32)
    L=C.shape[1]
    z=jnp.zeros((H,H),jnp.float32)
    top=C[:H]; bot=jnp.concatenate([C[H:,H:],z],axis=1)
    D=top+bot
    n=H
    D=jnp.concatenate([D,z],axis=1)
    W=L+H
    lane=None
    while n>1:
        n//=2
        D=D[:n]+pltpu.roll(D[n:],W-n,1)
    return D[:,:L]


VM = pl.BlockSpec(memory_space=pltpu.VMEM)
ANY = pl.BlockSpec(memory_space=pl.ANY)
NC = 8
RA = 384
CH = 128
NA = RA // CH


def kernel(
    q_ref, k_ref, v_ref, t_ref, w_hbm, og_hbm,
    proj_ref, gq_ref, gk_ref, gv_ref, gf_ref,
    w, og, tb, xp, gp, sx, sg, yb_, ub_, yr, ur, st, rt, sf, rf,
    sp, r0, ra, rb, acc, dg, cv, go,
    lsem, ags, agr, sibs, sibr, sps, spr, ras, rar, rbs, rbr, a2s, a2r,
):
    mc = lax.axis_index("ctx")
    mt = lax.axis_index("tp")
    zh, x = mc // 4, mc % 4
    zl, y, co = mt // 8, (mt // 2) % 4, mt % 2
    yd = 1 - 2 * co
    yf, yb, yo = (y + yd + 4) % 4, (y - yd + 4) % 4, (y + 2) % 4
    zp = 1 - zl
    T = lambda z, yy: z * 8 + yy * 2 + co
    M = lambda z, yy: z * 4 + yy
    front, back = (mc, T(zl, yf)), (mc, T(zl, yb))
    zpar, sib = (mc, T(zp, y)), (mc, zl * 8 + y * 2 + 1 - co)
    peers = []
    for k in range(1, NC):
        pc = ((zh + k // 4) % 2) * 4 + (x + k % 4) % 4
        peers.append((k, pc, (pc, mt)))
    G = 4
    L = 512
    scale = 1.0 / math.sqrt(NC * L)

    barrier = pltpu.get_barrier_semaphore()
    partners = [front, back, zpar, sib] + [p[2] for p in peers]
    for d in partners:
        pl.semaphore_signal(barrier, inc=1, device_id=d, device_id_type=MESH)
    wcopy = pltpu.make_async_copy(w_hbm, w, lsem.at[0])
    wcopy.start()
    ocopy = pltpu.make_async_copy(og_hbm, og.at[mt], lsem.at[1])
    ocopy.start()

    def spread(dst, full):
        for r in range(NC):
            for g in range(G):
                for ib in range(2):
                    dst[r, g, 16 * ib : 16 * ib + 16, :] = full[
                        64 * r + 16 * g : 64 * r + 16 * g + 16, B * ib : B * ib + B
                    ]

    def joined(src):
        rows = []
        for r in range(NC):
            for g in range(G):
                rows.append(
                    jnp.concatenate([src[r, g, 0:16, :], src[r, g, 16:32, :]], axis=1)
                )
        return jnp.concatenate(rows, axis=0)

    spread(sx, (k_ref[...].astype(f32) * v_ref[...].astype(f32)).astype(bf).T)
    tt = (t_ref[...] * scale).T
    for r in range(NC):
        st[r, 0:G, :] = tt[G * r : G * r + G, :]
        st[r, G:8, :] = tt[G * r : G * r + G, :]
    pl.semaphore_wait(barrier, len(partners))

    def rc(src, dst, s, r, dev):
        c = pltpu.make_async_remote_copy(
            src_ref=src, dst_ref=dst, send_sem=s, recv_sem=r, device_id=dev, device_id_type=MESH
        )
        c.start()
        return c

    sent = []

    def ag(i, z, yy, lo, n, dev, src=None):
        slot = T(z, yy)
        if src is None:
            s = og.at[slot, pl.ds(lo, n), :]
        else:
            s = src.at[pl.ds(lo, n), :]
        c = rc(s, og.at[slot, pl.ds(lo, n), :], ags.at[i], agr.at[i], dev)
        sent.append(c)
        return c

    RB = L - RA
    m1 = ag(0, zl, y, RA, RB, front, og_hbm)
    m2 = ag(1, zl, y, RA, RB, back, og_hbm)
    m3 = ag(2, zl, y, 0, RA, front, og_hbm)
    m4 = ag(3, zl, y, 0, RA, back, og_hbm)

    def a2a(base, src, dst):
        out = []
        for k, pc, dev in peers:
            c = rc(src(pc), dst, a2s.at[base, k - 1], a2r.at[base, k - 1], dev)
            sent.append(c)
            out.append(c)
        return out

    at32 = lambda c, off: pl.ds(pl.multiple_of(32 * c + off, 32), 32)
    tcs = a2a(0, lambda pc: st.at[pc], rt.at[mc])
    xcs = a2a(1, lambda pc: sx.at[pc], xp.at[:, at32(mc, B), :])
    m5 = ag(4, zl, y, 0, RA, zpar, og_hbm)
    m6 = ag(5, zl, y, RA, RB, zpar, og_hbm)

    def sibsend(z, yy, src=None):
        slot = T(z, yy)
        m = M(z, yy)
        c = rc(og.at[slot] if src is None else src, og.at[slot], sibs.at[m], sibr.at[m], sib)
        sent.append(c)
        return c

    def sibwait(z, yy):
        slot = z * 8 + yy * 2 + 1 - co
        m = M(z, yy)
        pltpu.make_async_remote_copy(
            src_ref=og.at[slot], dst_ref=og.at[slot], send_sem=sibs.at[m], recv_sem=sibr.at[m],
            device_id=sib, device_id_type=MESH,
        ).wait_recv()

    sibsend(zl, y, og_hbm)

    xp[:, 0:B, :] = jnp.zeros((G, B, B), bf)
    gp[:, B : 2 * B, :] = jnp.zeros((G, B, B), bf)
    xp[:, at32(mc, B), :] = sx[mc]
    rt[mc] = st[mc]
    acc[...] = jnp.zeros(acc.shape, f32)

    m1.wait_recv()
    m7 = ag(6, zl, yb, RA, RB, front)
    m8 = ag(7, zl, yb, RA, RB, zpar)
    m2.wait_recv()
    m9 = ag(8, zl, yf, RA, RB, zpar)

    for c in tcs:
        c.wait_recv()
    for g in range(G):
        build_tb(tb, g, jnp.concatenate([rt[s, g : g + 1, :] for s in range(NC)], axis=1))
    m7.wait_recv()
    m10 = ag(9, zl, yo, RA, RB, zpar)
    m5.wait_recv()
    m11 = ag(10, zp, y, 0, RA, front)
    m12 = ag(11, zp, y, 0, RA, back)
    for c in xcs:
        c.wait_recv()

    def fwd(g, _):
        yb_[g] = conv_fwd(xp, tb, g).astype(bf)
        return 0

    lax.fori_loop(0, G, fwd, 0)
    ycs = a2a(2, lambda pc: yb_.at[:, at32(pc, 0), :], yr.at[mc])
    yr[mc] = yb_[:, at32(mc, 0), :]

    m3.wait_recv()
    m13 = ag(12, zl, yb, 0, RA, front)
    sibsend(zl, yb)
    m4.wait_recv()
    sibsend(zl, yf)

    wcopy.wait()
    ocopy.wait()

    def dstep(z, yy):
        sibwait(z, yy)
        m = M(z, yy)

        def half(h, _):
            rows = pl.ds(pl.multiple_of(h * B, B), B)
            nt = (((1,), (1,)), ((), ()))
            a = lax.dot_general(
                og[2 * m, rows, :], w[:, pl.ds(pl.multiple_of(m * 1024, 1024), 512)],
                nt, preferred_element_type=f32,
            )
            b = lax.dot_general(
                og[2 * m + 1, rows, :], w[:, pl.ds(pl.multiple_of(m * 1024 + 512, 512), 512)],
                nt, preferred_element_type=f32,
            )
            acc[rows, :] += a + b
            return 0

        lax.fori_loop(0, 2, half, 0)

    dstep(zl, y)
    m6.wait_recv()
    sibsend(zp, y)
    dstep(zl, yb)
    dstep(zl, yf)
    dstep(zp, y)

    for c in ycs:
        c.wait_recv()
    conv = joined(yr).T
    cv[...] = conv
    go[...] = (q_ref[...].astype(f32) * conv.astype(f32)).astype(bf)

    def psib(o, _):
        z = (zl + o % 2) % 2
        yy = (y + 2 + o // 2) % 4
        m = M(z, yy)
        cols = pl.ds(pl.multiple_of((2 * m + 1 - co) * 512, 512), 512)
        sp[m] = jnp.dot(go[...], w[:, cols], preferred_element_type=f32).astype(bf)
        rc(sp.at[m], r0.at[m], sps.at[m], spr.at[m], sib)
        return 0

    lax.fori_loop(0, 8, psib, 0)

    m11.wait_recv()
    m14 = ag(13, zp, yb, 0, RA, front)
    m8.wait_recv()
    sibsend(zp, yb)
    m12.wait_recv()
    m9.wait_recv()
    sibsend(zp, yf)
    m13.wait_recv()
    sibsend(zl, yo)
    dstep(zp, yb)
    dstep(zp, yf)
    dstep(zl, yo)

    def spdesc(m):
        return pltpu.make_async_remote_copy(
            src_ref=sp.at[m], dst_ref=r0.at[m], send_sem=sps.at[m], recv_sem=spr.at[m],
            device_id=sib, device_id_type=MESH,
        )

    def own(yy):
        def one(o, _):
            m = M((zl + o) % 2, yy)
            cols = pl.ds(pl.multiple_of((2 * m + co) * 512, 512), 512)
            spdesc(m).wait_recv()
            r0[m] = (
                jnp.dot(go[...], w[:, cols], preferred_element_type=f32) + r0[m].astype(f32)
            ).astype(bf)
            return 0

        lax.fori_loop(0, 2, one, 0)

    def sa(i, j, z, yy, dev):
        c = rc(r0.at[M(z, yy), pl.ds(CH * j, CH), :], ra.at[i, j], ras.at[i, j], rar.at[i, j], dev)
        sent.append(c)
        return c

    def sb(i, z, yy, dev):
        c = rc(r0.at[M(z, yy), pl.ds(RA, RB), :], rb.at[i], rbs.at[i], rbr.at[i], dev)
        sent.append(c)
        return c

    def add(z, yy, lo, n, *parts):
        rows = pl.ds(lo, n)
        m = M(z, yy)
        total = r0[m, rows, :].astype(f32)
        for p in parts:
            total = total + p.astype(f32)
        return total

    own(yo)
    b1 = sb(0, zp, yo, zpar)
    a1 = [sa(0, j, zl, yo, front) for j in range(NA)]
    a2 = [sa(1, j, zp, yo, front) for j in range(NA)]
    own(yb)
    b2 = sb(1, zp, yb, zpar)
    a3 = [sa(2, j, zl, yb, back) for j in range(NA)]
    a4 = [sa(3, j, zp, yb, back) for j in range(NA)]
    own(yf)
    b3 = sb(2, zp, yf, zpar)
    own(y)
    b4 = sb(3, zp, y, zpar)

    m14.wait_recv()
    m10.wait_recv()
    sibsend(zp, yo)
    dstep(zp, yo)
    dgv = acc[...].astype(bf)
    dg[...] = dgv
    spread(sg, (dgv.astype(f32) * q_ref[...].astype(f32)).astype(bf).T)
    gcs = a2a(3, lambda pc: sg.at[pc], gp.at[:, at32(mc, 0), :])
    gp[:, at32(mc, 0), :] = sg[mc]
    gq_ref[...] = (dg[...].astype(f32) * cv[...].astype(f32)).astype(bf)

    a5, a6, a7 = [], [], []
    for j in range(NA):
        a1[j].wait_recv()
        r0[M(zl, yf), pl.ds(CH * j, CH), :] = add(zl, yf, CH * j, CH, ra[0, j]).astype(bf)
        a5.append(sa(4, j, zl, yf, front))
    b1.wait_recv()
    r0[M(zl, yo), pl.ds(RA, RB), :] = add(zl, yo, RA, RB, rb[0]).astype(bf)
    b5 = sb(4, zl, yo, front)
    for j in range(NA):
        a2[j].wait_recv()
        r0[M(zp, yf), pl.ds(CH * j, CH), :] = add(zp, yf, CH * j, CH, ra[1, j]).astype(bf)
        a6.append(sa(5, j, zp, yf, front))
    b2.wait_recv()
    r0[M(zl, yb), pl.ds(RA, RB), :] = add(zl, yb, RA, RB, rb[1]).astype(bf)
    b6 = sb(5, zl, yb, back)

    for c in gcs:
        c.wait_recv()

    def bwd(g, _):
        ub_[g] = conv_bwd(gg_of(gp, g), tmat(tb, g)).astype(bf)
        return 0

    lax.fori_loop(0, G, bwd, 0)
    ucs = a2a(4, lambda pc: ub_.at[:, at32(pc, 0), :], ur.at[mc])
    ur[mc] = ub_[:, at32(mc, 0), :]

    b3.wait_recv()
    b5.wait_recv()
    r0[M(zl, yf), pl.ds(RA, RB), :] = add(zl, yf, RA, RB, rb[2], rb[4]).astype(bf)
    b7 = sb(6, zl, yf, front)

    for g in range(G):
        row = filt_grad(xp[g, B : 2 * B, :], gg_of(gp, g)) * scale
        for r in range(NC):
            sf[r, g : g + 1, :] = row[:, L * r : L * r + L]
            sf[r, G + g : G + g + 1, :] = row[:, L * r : L * r + L]
    fcs = a2a(5, lambda pc: sf.at[pc], rf.at[mc])
    rf[mc] = sf[mc]

    for j in range(NA):
        a4[j].wait_recv()
        a6[j].wait_recv()
        r0[M(zp, y), pl.ds(CH * j, CH), :] = add(zp, y, CH * j, CH, ra[3, j], ra[5, j]).astype(bf)
        a7.append(sa(6, j, zp, y, zpar))

    for c in ucs:
        c.wait_recv()
    u = joined(ur).T.astype(f32)
    gk_ref[...] = (u * v_ref[...].astype(f32)).astype(bf)
    gv_ref[...] = (u * k_ref[...].astype(f32)).astype(bf)
    for c in fcs:
        c.wait_recv()
    gf_ref[...] = jnp.concatenate([rf[s, 0:G, :] for s in range(NC)], axis=0).T

    b4.wait_recv()
    b6.wait_recv()
    b7.wait_recv()
    proj_ref[pl.ds(RA, RB), :] = add(zl, y, RA, RB, rb[3], rb[5], rb[6]).astype(bf)
    for j in range(NA):
        a3[j].wait_recv()
        a5[j].wait_recv()
        a7[j].wait_recv()
        proj_ref[pl.ds(CH * j, CH), :] = add(
            zl, y, CH * j, CH, ra[2, j], ra[4, j], ra[6, j]
        ).astype(bf)

    for c in sent:
        c.wait_send()

    def drain(m, _):
        spdesc(m).wait_send()
        return 0

    lax.fori_loop(0, 8, drain, 0)


def local(query_gate, key_gate, value_input, filter_taps, out_weight, out_grad):
    L, D = query_gate.shape
    G = 4
    blk = jax.ShapeDtypeStruct((L, D), bf)
    vm = pltpu.VMEM
    dma = pltpu.SemaphoreType.DMA
    return pl.pallas_call(
        kernel,
        in_specs=[VM, VM, VM, VM, ANY, ANY],
        out_specs=(VM,) * 5,
        out_shape=(blk, blk, blk, blk, jax.ShapeDtypeStruct(filter_taps.shape, f32)),
        scratch_shapes=[
            vm(out_weight.shape, bf),
            vm((16, L, D), bf),
            vm((G, H, NC * L + 2 * H), bf),
            vm((G, 2 * B, B), bf),
            vm((G, 2 * B, B), bf),
            vm((NC, G, 32, B), bf),
            vm((NC, G, 32, B), bf),
            vm((G, B, B), bf),
            vm((G, B, B), bf),
            vm((NC, G, 32, B), bf),
            vm((NC, G, 32, B), bf),
            vm((NC, 8, L), f32),
            vm((NC, 8, L), f32),
            vm((NC, 8, L), f32),
            vm((NC, 8, L), f32),
            vm((8, L, D), bf),
            vm((8, L, D), bf),
            vm((7, NA, CH, D), bf),
            vm((7, L - RA, D), bf),
            vm((L, D), f32),
            vm((L, D), bf),
            vm((L, D), bf),
            vm((L, D), bf),
            dma((2,)),
            dma((14,)), dma((14,)),
            dma((8,)), dma((8,)),
            dma((8,)), dma((8,)),
            dma((7, NA)), dma((7, NA)),
            dma((7,)), dma((7,)),
            dma((6, NC - 1)), dma((6, NC - 1)),
        ],
        compiler_params=pltpu.CompilerParams(
            collective_id=0, has_side_effects=True, vmem_limit_bytes=62 << 20
        ),
        name="hyena",
    )(query_gate, key_gate, value_input, filter_taps, out_weight, out_grad)


def solution(mesh):
    spec = P("ctx", "tp")
    return jax.shard_map(
        local,
        mesh=mesh,
        in_specs=(spec, spec, spec, spec, P("tp", None), spec),
        out_specs=(spec,) * 5,
        check_vma=False,
    )
```

time: 167 us -> 112 us (0.67); the launches traced: 164 us -> 111 us
  Pallas kernels: 17.4 us -> 99.5 us
  waiting for transfers between devices: 51.1 us -> 0 us
  starting transfers between devices: 21.8 us -> 0 us
  matrix products: 20.6 us -> 0 us
  blocking collectives: 20.4 us -> 0 us
  between operations: 14.1 us -> 0.64 us
  local copies, waits for them, and re-layouts: 15.1 us -> 10.8 us
  other arithmetic: 3.7 us -> 0 us
    pallas_call x2 -> x1, Pallas kernels: 17.4 us -> 99.5 us  [local(): pl.pallas_call(kernel, in_specs=[VM, VM, VM, VM, ANY, ANY], out_specs=(VM...]
    all_to_all x5 -> x0, waiting for transfers between devices: 47.6 us -> none  [the longest x2 25.4 us: gather(): v = lax.all_to_all(v, 'ctx', 0, 0, tiled=True)]
    all_to_all x5 -> x0, starting transfers between devices: 21.7 us -> none  [the longest x1 7.7 us: scatter(): v = lax.all_to_all(v, 'ctx', 0, 0, tiled=True)]
    dot_general x2 -> x0, matrix products: 20.6 us -> none  [the longest x1 10.3 us: local(): jnp.einsum('tk,ck->tc', lax.all_gather(out_grad, 'tp', axis=1, tiled=True...]
    all_to_all x1 -> x0, blocking collectives: 20.4 us -> none  [scatter(): v = lax.all_to_all(v, 'ctx', 0, 0, tiled=True)]
    reshape x7 -> x0, local copies, waits for them, and re-layouts: 6.28 us -> none  [the longest x4 5.39 us: gather(): v.reshape(G, n, nb, per, B).transpose(1, 0, 3, 2, 4)]
    unnamed x10 -> x5, local copies, waits for them, and re-layouts: 6.37 us -> 9.15 us
    reduce_scatter x1 -> x0, waiting for transfers between devices: 2.77 us -> none  [local(): lax.psum_scatter(partial_value.astype(bf), 'tp', scatter_dimension=1, til...]
  transfers between devices with their start and end apart: 7 -> 0, of which waited for: 6 -> 0; matrix products, arithmetic and copies ran while one was open for 24% -> 0% of each run, Pallas kernels for 11% -> 0%
where the time goes in v2:
time: 112 us; the launch traced here: 111 us
  Pallas kernels  99.5 us (89%)
  local copies, waits for them, and re-layouts  10.8 us (10%)
    pallas_call x1, Pallas kernels, local(): pl.pallas_call(kernel, in_specs=[VM, VM, VM, VM, ANY, ANY], out_specs=(VM...  99.5 us
    unnamed x5, local copies, waits for them, and re-layouts  9.15 us

profile of v2, /device:TPU:0, one launch (start us, length us, event | category | flops | bytes accessed | tf_op | source)
XLA Modules:
  0.0 111.0 jit_solution(14727491126939478387)
XLA Ops:
  0.6 1.7 %copy.11.t_ref = f32[512,32]{1,0:T(8,128)} copy(f32[512,32]{0,1:T(8,128)} %param.9) | data formatting | bytes 131072 | tf_op args[3]
  2.3 99.5 %hyena.1 = (bf16[512,512]{1,0:T(8,128)(2,1)}, bf16[512,512]{1,0:T(8,128)(2,1)}, bf16[512,512]{1,0:T(8,128)(2,1)}, bf16[512,512]{1,0:T(8,128)(2,1)}, f32[512,32]{1,0:T(8,128)}) custom-call(bf16[512,512]{1,0:T(8,128)(2,1)} %q_ref.1, bf16[512,512]{1,0:T(8,128)(2,1)} %k_ref.1, bf16[512,512]{1,0:T(8,128)(2,1)} %v_ref.1, f32[512,32]{1,0:T(8,128)} %copy.11.t_ref, ...), custom_call_target="tpu_custom_call" | custom-call | tf_op jit(solution)/shard_map/hyena/pallas_call | solution.py:416
  101.8 1.7 %copy.12 = f32[512,32]{0,1:T(8,128)} copy(f32[512,32]{1,0:T(8,128)} %get-tuple-element.9) | data formatting | bytes 131072 | tf_op jit(solution)/shard_map/hyena/pallas_call | solution.py:416
  103.5 1.9 %copy.17 = bf16[512,512]{1,0:T(8,128)(2,1)} copy(bf16[512,512]{1,0:T(8,128)(2,1)} %get-tuple-element.15) | data formatting | bytes 1048576
  105.4 1.9 %copy.18 = bf16[512,512]{1,0:T(8,128)(2,1)} copy(bf16[512,512]{1,0:T(8,128)(2,1)} %get-tuple-element.16) | data formatting | bytes 1048576
  107.2 1.9 %copy.19 = bf16[512,512]{1,0:T(8,128)(2,1)} copy(bf16[512,512]{1,0:T(8,128)(2,1)} %get-tuple-element.17) | data formatting | bytes 1048576
  109.1 1.9 %copy.20 = bf16[512,512]{1,0:T(8,128)(2,1)} copy(bf16[512,512]{1,0:T(8,128)(2,1)} %get-tuple-element.18) | data formatting | bytes 1048576

commit v3 on v2

--- a/solution.py
+++ b/solution.py
@@ -58,11 +58,12 @@
 
 
 def kernel(
-    q_ref, k_ref, v_ref, t_ref, w_hbm, og_hbm,
+    q_hbm, k_hbm, v_hbm, t_hbm, w_hbm, og_hbm,
+    proj_out, gq_out, gk_out, gv_out, gf_out,
+    w, og, tb, xp, gp, sx, sg, yb_, ub_, yr, ur, st, rt, sf, rf,
+    sp, r0, ra, rb, acc, dg, cv, go, q_ref, k_ref, v_ref, t_ref,
     proj_ref, gq_ref, gk_ref, gv_ref, gf_ref,
-    w, og, tb, xp, gp, sx, sg, yb_, ub_, yr, ur, st, rt, sf, rf,
-    sp, r0, ra, rb, acc, dg, cv, go,
-    lsem, ags, agr, sibs, sibr, sps, spr, ras, rar, rbs, rbr, a2s, a2r,
+    lsem, osem, ags, agr, sibs, sibr, sps, spr, ras, rar, rbs, rbr, a2s, a2r,
 ):
     mc = lax.axis_index("ctx")
     mt = lax.axis_index("tp")
@@ -81,16 +82,25 @@
         peers.append((k, pc, (pc, mt)))
     G = 4
     L = 512
+    RB = L - RA
     scale = 1.0 / math.sqrt(NC * L)
 
     barrier = pltpu.get_barrier_semaphore()
     partners = [front, back, zpar, sib] + [p[2] for p in peers]
     for d in partners:
         pl.semaphore_signal(barrier, inc=1, device_id=d, device_id_type=MESH)
-    wcopy = pltpu.make_async_copy(w_hbm, w, lsem.at[0])
-    wcopy.start()
-    ocopy = pltpu.make_async_copy(og_hbm, og.at[mt], lsem.at[1])
-    ocopy.start()
+
+    def lc(src, dst, sem):
+        c = pltpu.make_async_copy(src, dst, sem)
+        c.start()
+        return c
+
+    tcopy = lc(t_hbm, t_ref, lsem.at[0])
+    kcopy = lc(k_hbm, k_ref, lsem.at[1])
+    vcopy = lc(v_hbm, v_ref, lsem.at[2])
+    qcopy = lc(q_hbm, q_ref, lsem.at[3])
+    ocopy = lc(og_hbm, og.at[mt], lsem.at[4])
+    wcopy = lc(w_hbm, w, lsem.at[5])
 
     def spread(dst, full):
         for r in range(NC):
@@ -109,13 +119,6 @@
                 )
         return jnp.concatenate(rows, axis=0)
 
-    spread(sx, (k_ref[...].astype(f32) * v_ref[...].astype(f32)).astype(bf).T)
-    tt = (t_ref[...] * scale).T
-    for r in range(NC):
-        st[r, 0:G, :] = tt[G * r : G * r + G, :]
-        st[r, G:8, :] = tt[G * r : G * r + G, :]
-    pl.semaphore_wait(barrier, len(partners))
-
     def rc(src, dst, s, r, dev):
         c = pltpu.make_async_remote_copy(
             src_ref=src, dst_ref=dst, send_sem=s, recv_sem=r, device_id=dev, device_id_type=MESH
@@ -125,21 +128,21 @@
 
     sent = []
 
-    def ag(i, z, yy, lo, n, dev, src=None):
+    def ag(i, z, yy, lo, n, dev, src=None, j=0):
         slot = T(z, yy)
         if src is None:
             s = og.at[slot, pl.ds(lo, n), :]
         else:
             s = src.at[pl.ds(lo, n), :]
-        c = rc(s, og.at[slot, pl.ds(lo, n), :], ags.at[i], agr.at[i], dev)
+        c = rc(s, og.at[slot, pl.ds(lo, n), :], ags.at[i, j], agr.at[i, j], dev)
         sent.append(c)
         return c
 
-    RB = L - RA
-    m1 = ag(0, zl, y, RA, RB, front, og_hbm)
-    m2 = ag(1, zl, y, RA, RB, back, og_hbm)
-    m3 = ag(2, zl, y, 0, RA, front, og_hbm)
-    m4 = ag(3, zl, y, 0, RA, back, og_hbm)
+    def aga(i, z, yy, dev, j, src=None):
+        return ag(i, z, yy, CH * j, CH, dev, src, j)
+
+    def agb(i, z, yy, dev, src=None):
+        return ag(i, z, yy, RA, RB, dev, src)
 
     def a2a(base, src, dst):
         out = []
@@ -149,11 +152,12 @@
             out.append(c)
         return out
 
+    def recv(cs):
+        for c in cs:
+            c.wait_recv()
+
     at32 = lambda c, off: pl.ds(pl.multiple_of(32 * c + off, 32), 32)
-    tcs = a2a(0, lambda pc: st.at[pc], rt.at[mc])
-    xcs = a2a(1, lambda pc: sx.at[pc], xp.at[:, at32(mc, B), :])
-    m5 = ag(4, zl, y, 0, RA, zpar, og_hbm)
-    m6 = ag(5, zl, y, RA, RB, zpar, og_hbm)
+    hf = lambda h: pl.ds(2 * h, 2)
 
     def sibsend(z, yy, src=None):
         slot = T(z, yy)
@@ -170,6 +174,27 @@
             device_id=sib, device_id_type=MESH,
         ).wait_recv()
 
+    pl.semaphore_wait(barrier, len(partners))
+    J = range(NA)
+    m5 = [aga(4, zl, y, zpar, 0, og_hbm)]
+    m1 = agb(0, zl, y, front, og_hbm)
+    m2 = agb(1, zl, y, back, og_hbm)
+    m3 = [aga(2, zl, y, front, j, og_hbm) for j in J]
+    m4 = [aga(3, zl, y, back, j, og_hbm) for j in J]
+    tcopy.wait()
+    for r in range(NC):
+        blk = t_ref[G * r : G * r + G, :] * scale
+        st[r, 0:G, :] = blk
+        st[r, G:8, :] = blk
+    tcs = a2a(0, lambda pc: st.at[pc], rt.at[mc])
+    kcopy.wait()
+    vcopy.wait()
+    spread(sx, (k_ref[...].astype(f32) * v_ref[...].astype(f32)).astype(bf).T)
+    xcs = [
+        a2a(1 + h, lambda pc, h=h: sx.at[pc, hf(h)], xp.at[hf(h), at32(mc, B), :]) for h in (0, 1)
+    ]
+    for j in range(1, NA):
+        m5.append(aga(4, zl, y, zpar, j, og_hbm))
     sibsend(zl, y, og_hbm)
 
     xp[:, 0:B, :] = jnp.zeros((G, B, B), bf)
@@ -178,40 +203,48 @@
     rt[mc] = st[mc]
     acc[...] = jnp.zeros(acc.shape, f32)
 
+    m5[0].wait_recv()
+    m11 = [aga(10, zp, y, front, 0)]
+    m12 = [aga(11, zp, y, back, 0)]
     m1.wait_recv()
-    m7 = ag(6, zl, yb, RA, RB, front)
-    m8 = ag(7, zl, yb, RA, RB, zpar)
-    m2.wait_recv()
-    m9 = ag(8, zl, yf, RA, RB, zpar)
-
-    for c in tcs:
-        c.wait_recv()
+    m7 = agb(6, zl, yb, front)
+    recv(tcs)
     for g in range(G):
         build_tb(tb, g, jnp.concatenate([rt[s, g : g + 1, :] for s in range(NC)], axis=1))
-    m7.wait_recv()
-    m10 = ag(9, zl, yo, RA, RB, zpar)
-    m5.wait_recv()
-    m11 = ag(10, zp, y, 0, RA, front)
-    m12 = ag(11, zp, y, 0, RA, back)
-    for c in xcs:
-        c.wait_recv()
 
     def fwd(g, _):
         yb_[g] = conv_fwd(xp, tb, g).astype(bf)
         return 0
 
-    lax.fori_loop(0, G, fwd, 0)
-    ycs = a2a(2, lambda pc: yb_.at[:, at32(pc, 0), :], yr.at[mc])
+    ycs = []
+    for h in (0, 1):
+        recv(xcs[h])
+        lax.fori_loop(2 * h, 2 * h + 2, fwd, 0)
+        ycs.append(
+            a2a(3 + h, lambda pc, h=h: yb_.at[hf(h), at32(pc, 0), :], yr.at[mc, hf(h)])
+        )
+        if h == 0:
+            for j in range(1, NA):
+                m5[j].wait_recv()
+                m11.append(aga(10, zp, y, front, j))
+                m12.append(aga(11, zp, y, back, j))
     yr[mc] = yb_[:, at32(mc, 0), :]
-
-    m3.wait_recv()
-    m13 = ag(12, zl, yb, 0, RA, front)
+    m6 = agb(5, zl, y, zpar, og_hbm)
+    m8 = agb(7, zl, yb, zpar)
+    m2.wait_recv()
+    m9 = agb(8, zl, yf, zpar)
+
+    m13 = []
+    for j in J:
+        m3[j].wait_recv()
+        m13.append(aga(12, zl, yb, front, j))
     sibsend(zl, yb)
-    m4.wait_recv()
+    recv(m4)
     sibsend(zl, yf)
 
     wcopy.wait()
     ocopy.wait()
+    qcopy.wait()
 
     def dstep(z, yy):
         sibwait(z, yy)
@@ -234,20 +267,23 @@
         lax.fori_loop(0, 2, half, 0)
 
     dstep(zl, y)
-    m6.wait_recv()
-    sibsend(zp, y)
+    m7.wait_recv()
+    m10 = agb(9, zl, yo, zpar)
+    m14 = [None] * NA
+    for j in range(NA - 1):
+        m11[j].wait_recv()
+        m14[j] = aga(13, zp, yb, front, j)
     dstep(zl, yb)
     dstep(zl, yf)
-    dstep(zp, y)
-
-    for c in ycs:
-        c.wait_recv()
+
+    recv(ycs[0])
+    recv(ycs[1])
     conv = joined(yr).T
     cv[...] = conv
     go[...] = (q_ref[...].astype(f32) * conv.astype(f32)).astype(bf)
 
     def psib(o, _):
-        z = (zl + o % 2) % 2
+        z = (zp + o % 2) % 2
         yy = (y + 2 + o // 2) % 4
         m = M(z, yy)
         cols = pl.ds(pl.multiple_of((2 * m + 1 - co) * 512, 512), 512)
@@ -255,20 +291,12 @@
         rc(sp.at[m], r0.at[m], sps.at[m], spr.at[m], sib)
         return 0
 
-    lax.fori_loop(0, 8, psib, 0)
-
-    m11.wait_recv()
-    m14 = ag(13, zp, yb, 0, RA, front)
-    m8.wait_recv()
-    sibsend(zp, yb)
-    m12.wait_recv()
-    m9.wait_recv()
-    sibsend(zp, yf)
-    m13.wait_recv()
-    sibsend(zl, yo)
-    dstep(zp, yb)
-    dstep(zp, yf)
-    dstep(zl, yo)
+    lax.fori_loop(0, 4, psib, 0)
+    m11[NA - 1].wait_recv()
+    m14[NA - 1] = aga(13, zp, yb, front, NA - 1)
+    m6.wait_recv()
+    sibsend(zp, y)
+    lax.fori_loop(4, 8, psib, 0)
 
     def spdesc(m):
         return pltpu.make_async_remote_copy(
@@ -278,7 +306,7 @@
 
     def own(yy):
         def one(o, _):
-            m = M((zl + o) % 2, yy)
+            m = M((zp + o) % 2, yy)
             cols = pl.ds(pl.multiple_of((2 * m + co) * 512, 512), 512)
             spdesc(m).wait_recv()
             r0[m] = (
@@ -306,96 +334,120 @@
             total = total + p.astype(f32)
         return total
 
+    def put(z, yy, lo, n, *parts):
+        r0[M(z, yy), pl.ds(lo, n), :] = add(z, yy, lo, n, *parts).astype(bf)
+
     own(yo)
+    a2 = [sa(1, j, zp, yo, front) for j in J]
     b1 = sb(0, zp, yo, zpar)
-    a1 = [sa(0, j, zl, yo, front) for j in range(NA)]
-    a2 = [sa(1, j, zp, yo, front) for j in range(NA)]
+    m8.wait_recv()
+    sibsend(zp, yb)
+    m9.wait_recv()
+    recv(m12)
+    sibsend(zp, yf)
     own(yb)
+    a4 = [sa(3, j, zp, yb, back) for j in J]
     b2 = sb(1, zp, yb, zpar)
-    a3 = [sa(2, j, zl, yb, back) for j in range(NA)]
-    a4 = [sa(3, j, zp, yb, back) for j in range(NA)]
+    recv(m13)
+    sibsend(zl, yo)
+    dstep(zp, y)
+    dstep(zp, yb)
+    dstep(zp, yf)
     own(yf)
     b3 = sb(2, zp, yf, zpar)
+    dstep(zl, yo)
+    recv(m14)
+    m10.wait_recv()
+    sibsend(zp, yo)
     own(y)
     b4 = sb(3, zp, y, zpar)
-
-    m14.wait_recv()
-    m10.wait_recv()
-    sibsend(zp, yo)
     dstep(zp, yo)
     dgv = acc[...].astype(bf)
     dg[...] = dgv
     spread(sg, (dgv.astype(f32) * q_ref[...].astype(f32)).astype(bf).T)
-    gcs = a2a(3, lambda pc: sg.at[pc], gp.at[:, at32(mc, 0), :])
+    gcs = [
+        a2a(5 + h, lambda pc, h=h: sg.at[pc, hf(h)], gp.at[hf(h), at32(mc, 0), :]) for h in (0, 1)
+    ]
+    a1 = [sa(0, j, zl, yo, front) for j in J]
     gp[:, at32(mc, 0), :] = sg[mc]
     gq_ref[...] = (dg[...].astype(f32) * cv[...].astype(f32)).astype(bf)
+    outs = [lc(gq_ref, gq_out, osem.at[0])]
 
     a5, a6, a7 = [], [], []
-    for j in range(NA):
-        a1[j].wait_recv()
-        r0[M(zl, yf), pl.ds(CH * j, CH), :] = add(zl, yf, CH * j, CH, ra[0, j]).astype(bf)
-        a5.append(sa(4, j, zl, yf, front))
+    for j in J:
+        a2[j].wait_recv()
+        put(zp, yf, CH * j, CH, ra[1, j])
+        a6.append(sa(5, j, zp, yf, front))
+    a3 = [sa(2, j, zl, yb, back) for j in J]
     b1.wait_recv()
-    r0[M(zl, yo), pl.ds(RA, RB), :] = add(zl, yo, RA, RB, rb[0]).astype(bf)
+    put(zl, yo, RA, RB, rb[0])
     b5 = sb(4, zl, yo, front)
-    for j in range(NA):
-        a2[j].wait_recv()
-        r0[M(zp, yf), pl.ds(CH * j, CH), :] = add(zp, yf, CH * j, CH, ra[1, j]).astype(bf)
-        a6.append(sa(5, j, zp, yf, front))
     b2.wait_recv()
-    r0[M(zl, yb), pl.ds(RA, RB), :] = add(zl, yb, RA, RB, rb[1]).astype(bf)
+    put(zl, yb, RA, RB, rb[1])
     b6 = sb(5, zl, yb, back)
-
-    for c in gcs:
-        c.wait_recv()
 
     def bwd(g, _):
         ub_[g] = conv_bwd(gg_of(gp, g), tmat(tb, g)).astype(bf)
         return 0
 
-    lax.fori_loop(0, G, bwd, 0)
-    ucs = a2a(4, lambda pc: ub_.at[:, at32(pc, 0), :], ur.at[mc])
-    ur[mc] = ub_[:, at32(mc, 0), :]
-
-    b3.wait_recv()
-    b5.wait_recv()
-    r0[M(zl, yf), pl.ds(RA, RB), :] = add(zl, yf, RA, RB, rb[2], rb[4]).astype(bf)
-    b7 = sb(6, zl, yf, front)
-
-    for g in range(G):
+    def fgrad(g):
         row = filt_grad(xp[g, B : 2 * B, :], gg_of(gp, g)) * scale
         for r in range(NC):
             sf[r, g : g + 1, :] = row[:, L * r : L * r + L]
             sf[r, G + g : G + g + 1, :] = row[:, L * r : L * r + L]
-    fcs = a2a(5, lambda pc: sf.at[pc], rf.at[mc])
-    rf[mc] = sf[mc]
-
-    for j in range(NA):
+
+    ucs = []
+    for h in (0, 1):
+        recv(gcs[h])
+        lax.fori_loop(2 * h, 2 * h + 2, bwd, 0)
+        ucs.append(
+            a2a(7 + h, lambda pc, h=h: ub_.at[hf(h), at32(pc, 0), :], ur.at[mc, hf(h)])
+        )
+    ur[mc] = ub_[:, at32(mc, 0), :]
+    fgrad(0)
+    for j in J:
+        a1[j].wait_recv()
+        put(zl, yf, CH * j, CH, ra[0, j])
+        a5.append(sa(4, j, zl, yf, front))
+    b3.wait_recv()
+    b5.wait_recv()
+    put(zl, yf, RA, RB, rb[2], rb[4])
+    b7 = sb(6, zl, yf, front)
+    fgrad(1)
+    for j in J:
         a4[j].wait_recv()
         a6[j].wait_recv()
-        r0[M(zp, y), pl.ds(CH * j, CH), :] = add(zp, y, CH * j, CH, ra[3, j], ra[5, j]).astype(bf)
+        put(zp, y, CH * j, CH, ra[3, j], ra[5, j])
         a7.append(sa(6, j, zp, y, zpar))
-
-    for c in ucs:
-        c.wait_recv()
+    fgrad(2)
+    fgrad(3)
+    fcs = a2a(9, lambda pc: sf.at[pc], rf.at[mc])
+    rf[mc] = sf[mc]
+
+    recv(ucs[0])
+    recv(ucs[1])
     u = joined(ur).T.astype(f32)
     gk_ref[...] = (u * v_ref[...].astype(f32)).astype(bf)
+    outs.append(lc(gk_ref, gk_out, osem.at[1]))
     gv_ref[...] = (u * k_ref[...].astype(f32)).astype(bf)
-    for c in fcs:
-        c.wait_recv()
-    gf_ref[...] = jnp.concatenate([rf[s, 0:G, :] for s in range(NC)], axis=0).T
-
+    outs.append(lc(gv_ref, gv_out, osem.at[2]))
+    recv(fcs)
+    for s in range(NC):
+        gf_ref[G * s : G * s + G, :] = rf[s, 0:G, :]
+    outs.append(lc(gf_ref, gf_out, osem.at[3]))
+
+    for j in J:
+        a3[j].wait_recv()
+        a7[j].wait_recv()
+        a5[j].wait_recv()
+        proj_ref[pl.ds(CH * j, CH), :] = add(
+            zl, y, CH * j, CH, ra[2, j], ra[4, j], ra[6, j]
+        ).astype(bf)
     b4.wait_recv()
     b6.wait_recv()
     b7.wait_recv()
     proj_ref[pl.ds(RA, RB), :] = add(zl, y, RA, RB, rb[3], rb[5], rb[6]).astype(bf)
-    for j in range(NA):
-        a3[j].wait_recv()
-        a5[j].wait_recv()
-        a7[j].wait_recv()
-        proj_ref[pl.ds(CH * j, CH), :] = add(
-            zl, y, CH * j, CH, ra[2, j], ra[4, j], ra[6, j]
-        ).astype(bf)
+    outs.append(lc(proj_ref, proj_out, osem.at[4]))
 
     for c in sent:
         c.wait_send()
@@ -405,6 +457,22 @@
         return 0
 
     lax.fori_loop(0, 8, drain, 0)
+    for c in outs:
+        c.wait()
+
+
+def handover(*refs):
+    n = 5
+    ins, outs, held, sem = refs[:n], refs[n : 2 * n], refs[2 * n : 3 * n], refs[-1]
+    first = [pltpu.make_async_copy(ins[i], held[i], sem.at[0, i]) for i in range(n)]
+    then = [pltpu.make_async_copy(held[i], outs[i], sem.at[1, i]) for i in range(n)]
+    for c in first:
+        c.start()
+    for i in range(n):
+        first[i].wait()
+        then[i].start()
+    for c in then:
+        c.wait()
 
 
 def local(query_gate, key_gate, value_input, filter_taps, out_weight, out_grad):
@@ -413,11 +481,12 @@
     blk = jax.ShapeDtypeStruct((L, D), bf)
     vm = pltpu.VMEM
     dma = pltpu.SemaphoreType.DMA
-    return pl.pallas_call(
+    shapes = (blk, blk, blk, blk, jax.ShapeDtypeStruct(filter_taps.shape[::-1], f32))
+    parts = pl.pallas_call(
         kernel,
-        in_specs=[VM, VM, VM, VM, ANY, ANY],
-        out_specs=(VM,) * 5,
-        out_shape=(blk, blk, blk, blk, jax.ShapeDtypeStruct(filter_taps.shape, f32)),
+        in_specs=[ANY] * 6,
+        out_specs=(ANY,) * 5,
+        out_shape=shapes,
         scratch_shapes=[
             vm(out_weight.shape, bf),
             vm((16, L, D), bf),
@@ -442,19 +511,37 @@
             vm((L, D), bf),
             vm((L, D), bf),
             vm((L, D), bf),
-            dma((2,)),
-            dma((14,)), dma((14,)),
+            vm((L, D), bf),
+            vm((L, D), bf),
+            vm((L, D), bf),
+            vm((filter_taps.shape[1], L), f32),
+            vm((L, D), bf),
+            vm((L, D), bf),
+            vm((L, D), bf),
+            vm((L, D), bf),
+            vm((filter_taps.shape[1], L), f32),
+            dma((6,)), dma((5,)),
+            dma((14, NA)), dma((14, NA)),
             dma((8,)), dma((8,)),
             dma((8,)), dma((8,)),
             dma((7, NA)), dma((7, NA)),
             dma((7,)), dma((7,)),
-            dma((6, NC - 1)), dma((6, NC - 1)),
+            dma((10, NC - 1)), dma((10, NC - 1)),
         ],
         compiler_params=pltpu.CompilerParams(
             collective_id=0, has_side_effects=True, vmem_limit_bytes=62 << 20
         ),
         name="hyena",
-    )(query_gate, key_gate, value_input, filter_taps, out_weight, out_grad)
+    )(query_gate, key_gate, value_input, filter_taps.T, out_weight, out_grad)
+    done = pl.pallas_call(
+        handover,
+        in_specs=[ANY] * 5,
+        out_specs=(ANY,) * 5,
+        out_shape=shapes,
+        scratch_shapes=[vm(a.shape, a.dtype) for a in shapes] + [dma((2, 5))],
+        name="handover",
+    )(*parts)
+    return (*done[:4], done[4].T)
 
 
 def solution(mesh):

time: 112 us -> 88.2 us (0.79)
  Pallas kernels: 99.5 us -> 87.2 us
  local copies, waits for them, and re-layouts: 10.8 us -> 0 us
    pallas_call x1 -> x2, Pallas kernels: 99.5 us -> 87.2 us  [the longest x1 84.8 us: local(): pl.pallas_call(kernel, in_specs=[ANY] * 6, out_specs=(ANY,) * 5, out_shap...]
    unnamed x5 -> x0, local copies, waits for them, and re-layouts: 9.15 us -> none
    pallas_call x1 -> x0, local copies, waits for them, and re-layouts: 1.69 us -> none  [local(): pl.pallas_call(kernel, in_specs=[VM, VM, VM, VM, ANY, ANY], out_specs=(VM...]
where the time goes in v3:
time: 88.2 us; the launch traced here: 88 us
  Pallas kernels  87.2 us (99%)
    pallas_call x1, Pallas kernels, local(): pl.pallas_call(kernel, in_specs=[ANY] * 6, out_specs=(ANY,) * 5, out_shap...  84.8 us
    pallas_call x1, Pallas kernels, local(): pl.pallas_call(handover, in_specs=[ANY] * 5, out_specs=(ANY,) * 5, out_sh...  2.45 us

profile of v3, /device:TPU:0, one launch (start us, length us, event | category | flops | bytes accessed | tf_op | source)
XLA Modules:
  0.0 88.0 jit_solution(3867792945163642749)
XLA Ops:
  0.6 84.8 %hyena.1 = (bf16[512,512]{1,0:T(8,128)(2,1)}, bf16[512,512]{1,0:T(8,128)(2,1)}, bf16[512,512]{1,0:T(8,128)(2,1)}, bf16[512,512]{1,0:T(8,128)(2,1)}, f32[32,512]{1,0:T(8,128)}) custom-call(bf16[512,512]{1,0:T(8,128)(2,1)} %q_hbm.1, bf16[512,512]{1,0:T(8,128)(2,1)} %k_hbm.1, bf16[512,512]{1,0:T(8,128)(2,1)} %v_hbm.1, f32[32,512]{1,0:T(8,128)} %bitcast.2, ...), custom_call_target="tpu_custom_call" | custom-call | tf_op jit(solution)/shard_map/hyena/pallas_call | solution.py:485
  85.4 2.4 %handover.1 = (bf16[512,512]{1,0:T(8,128)(2,1)}, bf16[512,512]{1,0:T(8,128)(2,1)}, bf16[512,512]{1,0:T(8,128)(2,1)}, bf16[512,512]{1,0:T(8,128)(2,1)}, f32[32,512]{1,0:T(8,128)}) custom-call(bf16[512,512]{1,0:T(8,128)(2,1)} %get-tuple-element.15.refs_0_, bf16[512,512]{1,0:T(8,128)(2,1)} %get-tuple-element.16.refs_1_, ...), custom_call_target="tpu_custom_call" | custom-call | tf_op jit(solution)/shard_map/handover/pallas_call | solution.py:536

commit v4 on v3

--- a/solution.py
+++ b/solution.py
@@ -95,9 +95,9 @@
         c.start()
         return c
 
-    tcopy = lc(t_hbm, t_ref, lsem.at[0])
     kcopy = lc(k_hbm, k_ref, lsem.at[1])
     vcopy = lc(v_hbm, v_ref, lsem.at[2])
+    tcopy = lc(t_hbm, t_ref, lsem.at[0])
     qcopy = lc(q_hbm, q_ref, lsem.at[3])
     ocopy = lc(og_hbm, og.at[mt], lsem.at[4])
     wcopy = lc(w_hbm, w, lsem.at[5])
@@ -217,8 +217,13 @@
         return 0
 
     ycs = []
+    m3[0].wait_recv()
+    m13 = [aga(12, zl, yb, front, 0)]
     for h in (0, 1):
         recv(xcs[h])
+        if h == 0:
+            m3[1].wait_recv()
+            m13.append(aga(12, zl, yb, front, 1))
         lax.fori_loop(2 * h, 2 * h + 2, fwd, 0)
         ycs.append(
             a2a(3 + h, lambda pc, h=h: yb_.at[hf(h), at32(pc, 0), :], yr.at[mc, hf(h)])
@@ -228,16 +233,15 @@
                 m5[j].wait_recv()
                 m11.append(aga(10, zp, y, front, j))
                 m12.append(aga(11, zp, y, back, j))
+            for j in range(2, NA):
+                m3[j].wait_recv()
+                m13.append(aga(12, zl, yb, front, j))
     yr[mc] = yb_[:, at32(mc, 0), :]
     m6 = agb(5, zl, y, zpar, og_hbm)
     m8 = agb(7, zl, yb, zpar)
     m2.wait_recv()
     m9 = agb(8, zl, yf, zpar)
 
-    m13 = []
-    for j in J:
-        m3[j].wait_recv()
-        m13.append(aga(12, zl, yb, front, j))
     sibsend(zl, yb)
     recv(m4)
     sibsend(zl, yf)
@@ -347,6 +351,7 @@
     sibsend(zp, yf)
     own(yb)
     a4 = [sa(3, j, zp, yb, back) for j in J]
+    a1 = [sa(0, j, zl, yo, front) for j in J]
     b2 = sb(1, zp, yb, zpar)
     recv(m13)
     sibsend(zl, yo)
@@ -368,7 +373,6 @@
     gcs = [
         a2a(5 + h, lambda pc, h=h: sg.at[pc, hf(h)], gp.at[hf(h), at32(mc, 0), :]) for h in (0, 1)
     ]
-    a1 = [sa(0, j, zl, yo, front) for j in J]
     gp[:, at32(mc, 0), :] = sg[mc]
     gq_ref[...] = (dg[...].astype(f32) * cv[...].astype(f32)).astype(bf)
     outs = [lc(gq_ref, gq_out, osem.at[0])]
@@ -378,13 +382,17 @@
         a2[j].wait_recv()
         put(zp, yf, CH * j, CH, ra[1, j])
         a6.append(sa(5, j, zp, yf, front))
-    a3 = [sa(2, j, zl, yb, back) for j in J]
     b1.wait_recv()
     put(zl, yo, RA, RB, rb[0])
     b5 = sb(4, zl, yo, front)
     b2.wait_recv()
     put(zl, yb, RA, RB, rb[1])
     b6 = sb(5, zl, yb, back)
+    a3 = [sa(2, j, zl, yb, back) for j in J]
+    for j in J:
+        a1[j].wait_recv()
+        put(zl, yf, CH * j, CH, ra[0, j])
+        a5.append(sa(4, j, zl, yf, front))
 
     def bwd(g, _):
         ub_[g] = conv_bwd(gg_of(gp, g), tmat(tb, g)).astype(bf)
@@ -403,22 +411,19 @@
         ucs.append(
             a2a(7 + h, lambda pc, h=h: ub_.at[hf(h), at32(pc, 0), :], ur.at[mc, hf(h)])
         )
+        if h == 0:
+            for j in J:
+                a4[j].wait_recv()
+                a6[j].wait_recv()
+                put(zp, y, CH * j, CH, ra[3, j], ra[5, j])
+                a7.append(sa(6, j, zp, y, zpar))
     ur[mc] = ub_[:, at32(mc, 0), :]
-    fgrad(0)
-    for j in J:
-        a1[j].wait_recv()
-        put(zl, yf, CH * j, CH, ra[0, j])
-        a5.append(sa(4, j, zl, yf, front))
     b3.wait_recv()
     b5.wait_recv()
     put(zl, yf, RA, RB, rb[2], rb[4])
     b7 = sb(6, zl, yf, front)
+    fgrad(0)
     fgrad(1)
-    for j in J:
-        a4[j].wait_recv()
-        a6[j].wait_recv()
-        put(zp, y, CH * j, CH, ra[3, j], ra[5, j])
-        a7.append(sa(6, j, zp, y, zpar))
     fgrad(2)
     fgrad(3)
     fcs = a2a(9, lambda pc: sf.at[pc], rf.at[mc])

time: 88.2 us -> 84 us (0.952)
  Pallas kernels: 87.2 us -> 82.6 us
    pallas_call x1, Pallas kernels: 84.8 us -> 80.1 us  [local(): pl.pallas_call(kernel, in_specs=[ANY] * 6, out_specs=(ANY,) * 5, out_shap...]
where the time goes in v4:
time: 84 us; the launch traced here: 83.2 us
  Pallas kernels  82.6 us (98%)
    pallas_call x1, Pallas kernels, local(): pl.pallas_call(kernel, in_specs=[ANY] * 6, out_specs=(ANY,) * 5, out_shap...  80.1 us
    pallas_call x1, Pallas kernels, local(): pl.pallas_call(handover, in_specs=[ANY] * 5, out_specs=(ANY,) * 5, out_sh...  2.45 us

profile of v4, /device:TPU:0, one launch (start us, length us, event | category | flops | bytes accessed | tf_op | source)
XLA Modules:
  0.0 83.2 jit_solution(11058593248290014091)
XLA Ops:
  0.6 80.1 %hyena.1 = (bf16[512,512]{1,0:T(8,128)(2,1)}, bf16[512,512]{1,0:T(8,128)(2,1)}, bf16[512,512]{1,0:T(8,128)(2,1)}, bf16[512,512]{1,0:T(8,128)(2,1)}, f32[32,512]{1,0:T(8,128)}) custom-call(bf16[512,512]{1,0:T(8,128)(2,1)} %q_hbm.1, bf16[512,512]{1,0:T(8,128)(2,1)} %k_hbm.1, bf16[512,512]{1,0:T(8,128)(2,1)} %v_hbm.1, f32[32,512]{1,0:T(8,128)} %bitcast.2, ...), custom_call_target="tpu_custom_call" | custom-call | tf_op jit(solution)/shard_map/hyena/pallas_call | solution.py:490
  80.8 2.4 %handover.1 = (bf16[512,512]{1,0:T(8,128)(2,1)}, bf16[512,512]{1,0:T(8,128)(2,1)}, bf16[512,512]{1,0:T(8,128)(2,1)}, bf16[512,512]{1,0:T(8,128)(2,1)}, f32[32,512]{1,0:T(8,128)}) custom-call(bf16[512,512]{1,0:T(8,128)(2,1)} %get-tuple-element.15.refs_0_, bf16[512,512]{1,0:T(8,128)(2,1)} %get-tuple-element.16.refs_1_, ...), custom_call_target="tpu_custom_call" | custom-call | tf_op jit(solution)/shard_map/handover/pallas_call | solution.py:541

commit v5 on v4

--- a/solution.py
+++ b/solution.py
@@ -55,6 +55,9 @@
 RA = 384
 CH = 128
 NA = RA // CH
+SA = 400
+SC = 80
+NS = SA // SC
 
 
 def kernel(
@@ -320,13 +323,16 @@
 
         lax.fori_loop(0, 2, one, 0)
 
+    JR = range(NS)
+    SB = L - SA
+
     def sa(i, j, z, yy, dev):
-        c = rc(r0.at[M(z, yy), pl.ds(CH * j, CH), :], ra.at[i, j], ras.at[i, j], rar.at[i, j], dev)
+        c = rc(r0.at[M(z, yy), pl.ds(SC * j, SC), :], ra.at[i, j], ras.at[i, j], rar.at[i, j], dev)
         sent.append(c)
         return c
 
     def sb(i, z, yy, dev):
-        c = rc(r0.at[M(z, yy), pl.ds(RA, RB), :], rb.at[i], rbs.at[i], rbr.at[i], dev)
+        c = rc(r0.at[M(z, yy), pl.ds(SA, SB), :], rb.at[i], rbs.at[i], rbr.at[i], dev)
         sent.append(c)
         return c
 
@@ -342,7 +348,7 @@
         r0[M(z, yy), pl.ds(lo, n), :] = add(z, yy, lo, n, *parts).astype(bf)
 
     own(yo)
-    a2 = [sa(1, j, zp, yo, front) for j in J]
+    a2 = [sa(1, j, zp, yo, front) for j in JR]
     b1 = sb(0, zp, yo, zpar)
     m8.wait_recv()
     sibsend(zp, yb)
@@ -350,8 +356,8 @@
     recv(m12)
     sibsend(zp, yf)
     own(yb)
-    a4 = [sa(3, j, zp, yb, back) for j in J]
-    a1 = [sa(0, j, zl, yo, front) for j in J]
+    a4 = [sa(3, j, zp, yb, back) for j in JR]
+    a1 = [sa(0, j, zl, yo, front) for j in JR]
     b2 = sb(1, zp, yb, zpar)
     recv(m13)
     sibsend(zl, yo)
@@ -378,20 +384,20 @@
     outs = [lc(gq_ref, gq_out, osem.at[0])]
 
     a5, a6, a7 = [], [], []
-    for j in J:
+    for j in JR:
         a2[j].wait_recv()
-        put(zp, yf, CH * j, CH, ra[1, j])
+        put(zp, yf, SC * j, SC, ra[1, j])
         a6.append(sa(5, j, zp, yf, front))
     b1.wait_recv()
-    put(zl, yo, RA, RB, rb[0])
+    put(zl, yo, SA, SB, rb[0])
     b5 = sb(4, zl, yo, front)
     b2.wait_recv()
-    put(zl, yb, RA, RB, rb[1])
+    put(zl, yb, SA, SB, rb[1])
     b6 = sb(5, zl, yb, back)
-    a3 = [sa(2, j, zl, yb, back) for j in J]
-    for j in J:
+    a3 = [sa(2, j, zl, yb, back) for j in JR]
+    for j in JR:
         a1[j].wait_recv()
-        put(zl, yf, CH * j, CH, ra[0, j])
+        put(zl, yf, SC * j, SC, ra[0, j])
         a5.append(sa(4, j, zl, yf, front))
 
     def bwd(g, _):
@@ -412,15 +418,15 @@
             a2a(7 + h, lambda pc, h=h: ub_.at[hf(h), at32(pc, 0), :], ur.at[mc, hf(h)])
         )
         if h == 0:
-            for j in J:
+            for j in JR:
                 a4[j].wait_recv()
                 a6[j].wait_recv()
-                put(zp, y, CH * j, CH, ra[3, j], ra[5, j])
+                put(zp, y, SC * j, SC, ra[3, j], ra[5, j])
                 a7.append(sa(6, j, zp, y, zpar))
     ur[mc] = ub_[:, at32(mc, 0), :]
     b3.wait_recv()
     b5.wait_recv()
-    put(zl, yf, RA, RB, rb[2], rb[4])
+    put(zl, yf, SA, SB, rb[2], rb[4])
     b7 = sb(6, zl, yf, front)
     fgrad(0)
     fgrad(1)
@@ -441,17 +447,17 @@
         gf_ref[G * s : G * s + G, :] = rf[s, 0:G, :]
     outs.append(lc(gf_ref, gf_out, osem.at[3]))
 
-    for j in J:
+    for j in JR:
         a3[j].wait_recv()
         a7[j].wait_recv()
         a5[j].wait_recv()
-        proj_ref[pl.ds(CH * j, CH), :] = add(
-            zl, y, CH * j, CH, ra[2, j], ra[4, j], ra[6, j]
+        proj_ref[pl.ds(SC * j, SC), :] = add(
+            zl, y, SC * j, SC, ra[2, j], ra[4, j], ra[6, j]
         ).astype(bf)
     b4.wait_recv()
     b6.wait_recv()
     b7.wait_recv()
-    proj_ref[pl.ds(RA, RB), :] = add(zl, y, RA, RB, rb[3], rb[5], rb[6]).astype(bf)
+    proj_ref[pl.ds(SA, SB), :] = add(zl, y, SA, SB, rb[3], rb[5], rb[6]).astype(bf)
     outs.append(lc(proj_ref, proj_out, osem.at[4]))
 
     for c in sent:
@@ -510,8 +516,8 @@
             vm((NC, 8, L), f32),
             vm((8, L, D), bf),
             vm((8, L, D), bf),
-            vm((7, NA, CH, D), bf),
-            vm((7, L - RA, D), bf),
+            vm((7, NS, SC, D), bf),
+            vm((7, L - SA, D), bf),
             vm((L, D), f32),
             vm((L, D), bf),
             vm((L, D), bf),
@@ -529,7 +535,7 @@
             dma((14, NA)), dma((14, NA)),
             dma((8,)), dma((8,)),
             dma((8,)), dma((8,)),
-            dma((7, NA)), dma((7, NA)),
+            dma((7, NS)), dma((7, NS)),
             dma((7,)), dma((7,)),
             dma((10, NC - 1)), dma((10, NC - 1)),
         ],

time: 84 us -> 83.6 us (level)
  no operation moved by 1% of the time
where the time goes in v5:
time: 83.6 us; the launch traced here: 83.5 us
  Pallas kernels  82.8 us (99%)
    pallas_call x1, Pallas kernels, local(): pl.pallas_call(kernel, in_specs=[ANY] * 6, out_specs=(ANY,) * 5, out_shap...  80.4 us
    pallas_call x1, Pallas kernels, local(): pl.pallas_call(handover, in_specs=[ANY] * 5, out_specs=(ANY,) * 5, out_sh...  2.45 us

profile of v5, /device:TPU:0, one launch (start us, length us, event | category | flops | bytes accessed | tf_op | source)
XLA Modules:
  0.0 83.5 jit_solution(13194407552664885070)
XLA Ops:
  0.6 80.4 %hyena.1 = (bf16[512,512]{1,0:T(8,128)(2,1)}, bf16[512,512]{1,0:T(8,128)(2,1)}, bf16[512,512]{1,0:T(8,128)(2,1)}, bf16[512,512]{1,0:T(8,128)(2,1)}, f32[32,512]{1,0:T(8,128)}) custom-call(bf16[512,512]{1,0:T(8,128)(2,1)} %q_hbm.1, bf16[512,512]{1,0:T(8,128)(2,1)} %k_hbm.1, bf16[512,512]{1,0:T(8,128)(2,1)} %v_hbm.1, f32[32,512]{1,0:T(8,128)} %bitcast.2, ...), custom_call_target="tpu_custom_call" | custom-call | tf_op jit(solution)/shard_map/hyena/pallas_call | solution.py:496
  81.0 2.4 %handover.1 = (bf16[512,512]{1,0:T(8,128)(2,1)}, bf16[512,512]{1,0:T(8,128)(2,1)}, bf16[512,512]{1,0:T(8,128)(2,1)}, bf16[512,512]{1,0:T(8,128)(2,1)}, f32[32,512]{1,0:T(8,128)}) custom-call(bf16[512,512]{1,0:T(8,128)(2,1)} %get-tuple-element.15.refs_0_, bf16[512,512]{1,0:T(8,128)(2,1)} %get-tuple-element.16.refs_1_, ...), custom_call_target="tpu_custom_call" | custom-call | tf_op jit(solution)/shard_map/handover/pallas_call | solution.py:547
